TPU v7x, 128 devices: a whole 4x4x4 slice. The times are simulated.
128 devices in a mesh: grp: 32 (over x_hi, z, y), tp: 4 (over x_lo, core).
Axes of the slice: x: 4 (x_hi: 2, x_lo: 2; x = x_hi * 2 + x_lo), y: 4, z: 4, core: 2. Of those that a mesh axis runs over, the one named last changes fastest.
Arguments:
- hidden_in: bfloat16 [512, 5120], P('grp', 'tp'), may hold values from -70 to 70
- cache_lengths: int32 [512], P('grp'), may hold values from 160 to 1280, as said below
- in_gain: float32 [5120], replicated, may hold values from 0.1 to 1.9
- post_gain: float32 [5120], replicated, may hold values from 0.1 to 1.9
- w_query: bfloat16 [5120, 2560], P(None, 'tp'), may hold values from -0.078125 to 0.078125
- b_query: float32 [2560], P('tp'), may hold values from -5 to 5
- b_key: float32 [512], P('tp'), may hold values from -5 to 5
- b_value: float32 [512], P('tp'), may hold values from -3 to 3
- w_out: bfloat16 [2560, 5120], P('tp'), may hold values from -0.75 to 0.75
- key_cache: bfloat16 [512, 4, 1280, 128], P('grp', 'tp'), may hold values from -500 to 500
- value_cache: bfloat16 [512, 4, 1280, 128], P('grp', 'tp'), may hold values from -6 to 6
- next_key_weight: bfloat16 [5120, 512], P(('grp', 'tp')), may hold values from -0.078125 to 0.078125
- next_w_value: bfloat16 [5120, 512], P(('grp', 'tp')), may hold values from -0.078125 to 0.078125
Outputs:
- attended: bfloat16 [512, 5120], P('grp', 'tp')
- normed: bfloat16 [512, 5120], P('grp', 'tp')
- key_weight_out: bfloat16 [5120, 512], P(None, 'tp')
- value_weight_out: bfloat16 [5120, 512], P(None, 'tp')
Inputs may be any that keep to these rules, and one draw needn't show every extreme that they name: `cache_lengths`: the number of cached positions of each row; the new token stands at that position; some row holds exactly 1280.
All inputs are finite; a program needn't handle non-finite values.
Results may differ from a plain program's by a relative error of at most 0.02.
Values may be sent and summed in bfloat16 or wider, within the bound.
A program may use at most 128 MiB of HBM per device.

v0:
```python
import jax
import jax.numpy as jnp
from jax import lax
from jax.sharding import PartitionSpec as P

HD = 128


NORM_EPS = 1e-06
ROPE_BASE = 1000000.0


def rotate_heads(vectors, positions):
    half_width = vectors.shape[-1] // 2
    exponent = jnp.arange(half_width, dtype=jnp.float32) * (-2.0 / vectors.shape[-1])
    frequency = jnp.power(ROPE_BASE, exponent)
    rotary_angles = positions.astype(jnp.float32)[:, None] * frequency[None, :]
    cosine = jnp.cos(rotary_angles)[:, None, :]
    sine_part = jnp.sin(rotary_angles)[:, None, :]
    first_half = vectors[..., :half_width]
    second_half = vectors[..., half_width:]
    return jnp.concatenate(
        [
            first_half * cosine - second_half * sine_part,
            second_half * cosine + first_half * sine_part,
        ],
        axis=-1,
    )


def shards(
    hidden_in,
    cache_lengths,
    in_gain,
    post_gain,
    w_query,
    b_query,
    b_key,
    b_value,
    w_out,
    key_cache,
    value_cache,
    next_key_weight,
    next_w_value,
):
    column_width = next_key_weight.shape[1] // lax.axis_size("tp")
    gathered = (
        lax.all_gather(next_key_weight, ("grp", "tp"), axis=0, tiled=True),
        lax.all_gather(next_w_value, ("grp", "tp"), axis=0, tiled=True),
    )
    weight_start = lax.axis_index("tp") * column_width
    key_out = lax.dynamic_slice_in_dim(gathered[0], weight_start, column_width, 1)
    value_out = lax.dynamic_slice_in_dim(gathered[1], weight_start, column_width, 1)
    full_rows = lax.all_gather(hidden_in, "tp", axis=1, tiled=True)
    rows_f32 = full_rows.astype(jnp.float32)
    inverse_in = lax.rsqrt(jnp.mean(rows_f32 * rows_f32, axis=-1, keepdims=True) + NORM_EPS)
    normed_in = (rows_f32 * inverse_in * in_gain).astype(jnp.bfloat16)
    batch_rows = hidden_in.shape[0]
    local_heads = w_query.shape[1] // HD
    device_groups = key_out.shape[1] // HD
    per_group = local_heads // device_groups
    query_raw = jnp.dot(normed_in, w_query, preferred_element_type=jnp.float32) + b_query
    key_raw = jnp.dot(normed_in, key_out, preferred_element_type=jnp.float32) + b_key
    value_raw = jnp.dot(normed_in, value_out, preferred_element_type=jnp.float32) + b_value
    queries = rotate_heads(query_raw.reshape(batch_rows, local_heads, HD), cache_lengths).astype(
        jnp.bfloat16
    )
    fresh_key = rotate_heads(key_raw.reshape(batch_rows, device_groups, HD), cache_lengths).astype(
        jnp.bfloat16
    )
    new_value = value_raw.reshape(batch_rows, device_groups, HD).astype(jnp.bfloat16)
    grouped_heads = queries.reshape(batch_rows, device_groups, per_group, HD)
    score_scale = HD ** (-0.5)
    scores = (
        jnp.einsum("bkgd,bkjd->bkgj", grouped_heads, key_cache, preferred_element_type=jnp.float32)
        * score_scale
    )
    own_score = (
        jnp.einsum("aerm,aem->aer", grouped_heads, fresh_key, preferred_element_type=jnp.float32)
        * score_scale
    )
    slot_count = key_cache.shape[2]
    in_cache = (jnp.arange(slot_count, dtype=jnp.int32)[None, :] < cache_lengths[:, None])[
        :, None, None, :
    ]
    peak_score = jnp.maximum(jnp.max(jnp.where(in_cache, scores, -jnp.inf), axis=-1), own_score)
    weights = jnp.where(in_cache, jnp.exp(scores - peak_score[..., None]), 0.0)
    own_weight = jnp.exp(own_score - peak_score)
    denominator = jnp.sum(weights, axis=-1) + own_weight
    probs = (weights / denominator[..., None]).astype(jnp.bfloat16)
    own_prob = (own_weight / denominator).astype(jnp.bfloat16)
    mixed = jnp.einsum("bkgj,bkjd->bkgd", probs, value_cache, preferred_element_type=jnp.float32)
    mixed = (
        mixed
        + own_prob.astype(jnp.float32)[..., None] * new_value.astype(jnp.float32)[:, :, None, :]
    )
    context = mixed.astype(jnp.bfloat16).reshape(batch_rows, local_heads * HD)
    partial_out = jnp.dot(context, w_out, preferred_element_type=jnp.float32)
    feature_width = hidden_in.shape[1]
    col_start = lax.axis_index("tp") * feature_width
    share = lax.psum_scatter(
        partial_out.astype(jnp.bfloat16), "tp", scatter_dimension=1, tiled=True
    )
    residual = (hidden_in.astype(jnp.float32) + share.astype(jnp.float32)).astype(jnp.bfloat16)
    resid_f32 = residual.astype(jnp.float32)
    square_total = lax.psum(jnp.sum(resid_f32 * resid_f32, axis=-1), "tp")
    inverse_post = lax.rsqrt(square_total / full_rows.shape[1] + NORM_EPS)
    gain_share = lax.dynamic_slice_in_dim(post_gain, col_start, feature_width, 0)
    normed = (resid_f32 * inverse_post[:, None] * gain_share).astype(jnp.bfloat16)
    return (share, normed, key_out, value_out)


def solution(mesh):
    in_specs = (
        P("grp", "tp"),
        P("grp"),
        P(),
        P(),
        P(None, "tp"),
        P("tp"),
        P("tp"),
        P("tp"),
        P("tp", None),
        P("grp", "tp", None, None),
        P("grp", "tp", None, None),
        P(("grp", "tp"), None),
        P(("grp", "tp"), None),
    )
    out_specs = (P("grp", "tp"), P("grp", "tp"), P(None, "tp"), P(None, "tp"))
    return jax.shard_map(shards, mesh=mesh, in_specs=in_specs, out_specs=out_specs, check_vma=False)
```

profile of v0, /device:TPU:1, one launch (start us, length us, event | category | flops | bytes accessed | tf_op | source)
XLA Modules:
  0.0 453.5 jit_solution(6415079955843221973)
XLA Ops:
  7.2 0.0 all-gather.3.cloned.1.call-start
  7.2 0.7 all-gather.3.cloned.1.call-update
  7.9 0.0 all-gather.5.cloned.1.call-start
  8.0 0.7 all-gather.5.cloned.1.call-update
  8.7 0.0 reduce-scatter.2.cloned.1.call-start
  8.7 0.7 convert_element_type.62
  9.4 7.0 %all_gather.9 = bf16[16,5120]{1,0:T(8,128)(2,1)S(1)} all-gather(bf16[16,1280]{1,0:T(8,128)(2,1)} %param.13), channel_id=1, replica_groups=mesh['grp'=32,'tp'=4] {'tp'}, dimensions={1}, use_global_device_ids=true | all-gather | bytes 204800 | tf_op jit(solution)/shard_map/all_gather | solution.py:54
  16.3 0.2 fusion.17
  16.5 3.9 convolution_add_fusion
  20.4 0.1 multiply_cosine_fusion.1
  20.5 0.1 subtract_convert_fusion
  20.6 0.1 iota_compare_fusion
  20.7 4.1 select_reduce_fusion
  24.8 188.1 %all-gather.3.cloned.1.call-done = bf16[5120,512]{1,0:T(8,128)(2,1)} async-done(((bf16[40,512]{1,0:T(8,128)(2,1)}), bf16[5120,512]{1,0:T(8,128)(2,1)}) %all-gather.3.cloned.1.call-update) | async-done | bytes 5242896 | tf_op jit(solution)/shard_map/all_gather | solution.py:48
  213.0 1.4 constant_dynamic-slice_fusion.1
  214.4 0.0 copy-start
  214.4 0.3 fusion.13
  214.7 0.1 fusion.41
  214.9 0.1 maximum_bitcast_fusion
  214.9 0.2 fusion.37
  215.2 0.3 fusion.16
  215.5 197.8 %all-gather.5.cloned.1.call-done = bf16[5120,512]{1,0:T(8,128)(2,1)} async-done(((bf16[40,512]{1,0:T(8,128)(2,1)}), bf16[5120,512]{1,0:T(8,128)(2,1)}) %all-gather.5.cloned.1.call-update) | async-done | bytes 5242896 | tf_op jit(solution)/shard_map/all_gather | solution.py:49
  413.3 1.4 constant_dynamic-slice_fusion
  414.8 0.3 fusion.15
  415.1 3.5 fusion.10
  418.6 4.5 convolution_convert_fusion
  423.1 0.0 reduce-scatter.2.cloned.1.call-update
  423.1 0.8 dynamic_slice.11
  423.9 15.5 %reduce-scatter.2.cloned.1.call-done = bf16[16,1280]{1,0:T(8,128)(2,1)} async-done(((bf16[16,5120]{1,0:T(8,128)(2,1)}), bf16[16,1280]{1,0:T(8,128)(2,1)}) %reduce-scatter.2.cloned.1.call-update) | async-done | bytes 40976 | tf_op jit(solution)/shard_map/reduce_scatter | solution.py:101
  439.4 0.9 fusion.24
  440.3 5.2 %psum.7 = f32[16]{0:T(128)S(1)} all-reduce(f32[16]{0:T(128)S(1)} %fusion.24), channel_id=1, replica_groups=mesh['grp'=32,'tp'=4] {'tp'}, use_global_device_ids=true, to_apply=%region_5.6 | all-reduce | flops 16 | bytes 128 | tf_op jit(solution)/shard_map/psum | solution.py:106
  445.5 1.5 fusion.26
  (19 shorter events, 0.1 us)
Async XLA Ops:
  7.2 13.5 %copy-start.6 = (s32[16]{0:T(128)S(1)}, s32[16]{0:T(128)}, u32[]{:S(2)}) copy-start(s32[16]{0:T(128)} %param.14) | copy-start | bytes 196
  7.2 205.8 %all-gather.3.cloned.1.call-start = ((), (), s32[]{:S(2)}) async-start(), calls=%async_computation.1 | async-start | bytes 5283840 | tf_op jit(solution)/shard_map/all_gather | solution.py:48
  7.9 405.4 %all-gather.5.cloned.1.call-start = ((), (), s32[]{:S(2)}) async-start(), calls=%async_computation.2 | async-start | bytes 5283840 | tf_op jit(solution)/shard_map/all_gather | solution.py:49
  8.7 430.7 %reduce-scatter.2.cloned.1.call-start = ((), (), s32[]{:S(2)}) async-start(), calls=%async_computation.3 | async-start | bytes 204800 | tf_op jit(solution)/shard_map/reduce_scatter | solution.py:101
  20.4 194.0 %copy-start.3 = (f32[5120]{0:T(1024)S(1)}, f32[5120]{0:T(1024)}, u32[]{:S(2)}) copy-start(f32[5120]{0:T(1024)} %param.15) | copy-start | bytes 61444
  20.4 194.0 %copy-start.4 = (f32[128]{0:T(128)S(1)}, f32[128]{0:T(128)}, u32[]{:S(2)}) copy-start(f32[128]{0:T(128)} %param.19) | copy-start | bytes 1540
  24.8 389.9 %copy-start.5 = (f32[128]{0:T(128)S(1)}, f32[128]{0:T(128)}, u32[]{:S(2)}) copy-start(f32[128]{0:T(128)} %param.20) | copy-start | bytes 1540
  214.4 204.2 %copy-start = (bf16[5120,128]{1,0:T(8,128)(2,1)}, bf16[5120,128]{1,0:T(8,128)(2,1)S(1)}, u32[]{:S(2)}) copy-start(bf16[5120,128]{1,0:T(8,128)(2,1)S(1)} %constant_dynamic-slice_fusion.1) | copy-start | bytes 3932164
  414.8 8.3 %copy-start.1 = (bf16[5120,128]{1,0:T(8,128)(2,1)}, bf16[5120,128]{1,0:T(8,128)(2,1)S(1)}, u32[]{:S(2)}) copy-start(bf16[5120,128]{1,0:T(8,128)(2,1)S(1)} %constant_dynamic-slice_fusion) | copy-start | bytes 3932164
  415.1 24.3 %copy-start.2 = (bf16[16,1280]{1,0:T(8,128)(2,1)S(1)}, bf16[16,1280]{1,0:T(8,128)(2,1)}, u32[]{:S(2)}) copy-start(bf16[16,1280]{1,0:T(8,128)(2,1)} %param.13) | copy-start | bytes 122884
Sparse Core Ops, SparseCore 0:
  9.7 203.1 all-gather.2
  214.7 198.6 all-gather.4
  423.2 16.1 reduce-scatter.1
where the time goes:
time: 454 us; the launch traced here: 453 us
  waiting for transfers between devices  403 us (89%)
  matrix products  16.8 us (4%)
  between operations  13.9 us (3%)
  blocking collectives  12.1 us (3%)
    all_gather x1, waiting for transfers between devices, shards(): lax.all_gather(next_w_value, ('grp', 'tp'), axis=0, tiled=True)  198 us
    all_gather x1, waiting for transfers between devices, shards(): lax.all_gather(next_key_weight, ('grp', 'tp'), axis=0, tiled=True)  188 us
    reduce_scatter x1, waiting for transfers between devices, shards(): lax.psum_scatter(partial_out.astype(jnp.bfloat16), 'tp', scatter_dimensio...  15.5 us
  transfers between devices with their start and end apart: 3, of which 3 were waited for; matrix products, arithmetic and copies ran while one was open for 3% of the time, Pallas kernels for 0%

commit v1 on v0

v1 whole, which is shorter than its diff:
```python
import functools
import math

import jax
import jax.numpy as jnp
from jax import lax
from jax.experimental import pallas as pl
from jax.experimental.pallas import tpu as pltpu
from jax.sharding import PartitionSpec as P

MESH = pl.DeviceIdType.MESH
F32 = jnp.float32
BF16 = jnp.bfloat16

D = 5120
HD = 128
ROWS = 16
HEADS = 5
CACHE = 1280
WIDTH = 1280
SHARD = 40
BLOCK = 160
CHUNK = 640
CHUNKS = 8
EPS = 1e-06
ROPE_BASE = 1000000.0
SCALE = HD ** (-0.5)

HIDDEN = 0
LINE = 3
GATHER = 17
SHARE = 57
STAT = 60
COPIES = 63
L_HID, L_LEN, L_IN, L_POST, L_BQ, L_BK, L_BV, L_OWNK, L_OWNV = range(9)
L_WQ = 9
L_KC = L_WQ + CHUNKS
L_VC = L_KC + 8
L_WO = L_VC + 8
LOCALS = L_WO + 4


def kernel(
    hid, lens, in_gain, post_gain, wq, bq, bk, bv, wo, kc, vc, nk, nv,
    att_out, norm_out, k_out, v_out,
    h_buf, len_s, ig, pg, bq_s, bk_s, bv_s, x_buf, wq_s, kc_s, vc_s, wo_s,
    n_buf, q_s, o_s, m_s, l_s, ctx_s, send_buf, r_buf, stat_send, stat_buf,
    lsem, ssem, rsem,
):
    g = lax.axis_index("grp")
    t = lax.axis_index("tp")
    xh, z, y = g // 16, (g // 4) % 4, g % 4

    def group(xh_, z_, y_):
        return xh_ * 16 + z_ * 4 + y_

    def local(src, dst, i):
        return pltpu.make_async_copy(src, dst, lsem.at[i])

    def remote(src, dst, i, dev):
        return pltpu.make_async_remote_copy(
            src_ref=src, dst_ref=dst, send_sem=ssem.at[i], recv_sem=rsem.at[i], device_id=dev, device_id_type=MESH
        )

    columns = pl.ds(pl.multiple_of(t * HD, HD), HD)
    local(hid, h_buf.at[t], L_HID).start()
    local(nk.at[:, columns], x_buf.at[0, xh, t], L_OWNK).start()
    local(nv.at[:, columns], x_buf.at[1, xh, t], L_OWNV).start()
    small = [
        local(lens, len_s, L_LEN),
        local(in_gain, ig, L_IN),
        local(post_gain, pg, L_POST),
        local(bq, bq_s, L_BQ),
        local(bk, bk_s, L_BK),
        local(bv, bv_s, L_BV),
    ]
    for c in small:
        c.start()

    line = [(dx, dt) for dx in (0, 1) for dt in range(4) if (dx, dt) != (0, 0)]
    barrier = pltpu.get_barrier_semaphore()
    partners = [(group((xh + dx) % 2, z, y), (t + dt) % 4) for dx, dt in line]
    partners += [(group(xh, z, (y + d) % 4), t) for d in (1, 3)]
    partners += [(group(xh, (z + d) % 4, y), t) for d in (1, 3)]
    for dev in partners:
        pl.semaphore_signal(barrier, inc=1, device_id=dev, device_id_type=MESH)

    def wq_copy(i):
        return local(wq.at[pl.ds(i * CHUNK, CHUNK)], wq_s.at[i], L_WQ + i)

    def kc_copy(p):
        return local(kc.at[pl.ds(2 * p, 2)], kc_s.at[pl.ds(2 * p, 2)], L_KC + p)

    def vc_copy(p):
        return local(vc.at[pl.ds(2 * p, 2)], vc_s.at[pl.ds(2 * p, 2)], L_VC + p)

    def wo_copy(i):
        return local(wo.at[:, pl.ds(pl.multiple_of(i * WIDTH, WIDTH), WIDTH)], wo_s.at[i], L_WO + i)

    pl.semaphore_wait(barrier, len(partners))

    line_copies = []
    for n, (dx, dt) in enumerate(line):
        to_t = (t + dt) % 4
        dev = (group((xh + dx) % 2, z, y), to_t)
        cols = pl.ds(pl.multiple_of(to_t * HD, HD), HD)
        for kv, src in ((0, nk), (1, nv)):
            c = remote(src.at[:, cols], x_buf.at[kv, xh, t], LINE + 2 * n + kv, dev)
            c.start()
            line_copies.append(c)
    hidden_copies = []
    for dt in (1, 2, 3):
        c = remote(hid, h_buf.at[t], HIDDEN + dt - 1, (g, (t + dt) % 4))
        c.start()
        hidden_copies.append(c)

    def start_all(make, count):
        def body(i, _):
            make(i).start()
            return 0

        lax.fori_loop(0, count, body, 0)

    start_all(wq_copy, CHUNKS)
    start_all(kc_copy, 8)
    start_all(vc_copy, 8)
    start_all(wo_copy, 4)

    for c in small:
        c.wait()
    row_ids = lax.broadcasted_iota(jnp.int32, (ROWS, HD), 0)
    lane_ids = lax.broadcasted_iota(jnp.int32, (ROWS, HD), 1)
    position = jnp.zeros((ROWS, HD), jnp.int32)
    for r in range(ROWS):
        position = jnp.where(row_ids == r, len_s[r], position)
    exponent = (lane_ids % (HD // 2)).astype(F32) * (-2.0 / HD * math.log(ROPE_BASE))
    angle = position.astype(F32) * jnp.exp(exponent)
    cosine = jnp.cos(angle)
    sine = jnp.where(lane_ids < HD // 2, -jnp.sin(angle), jnp.sin(angle))

    def rotate(v):
        return v * cosine + pltpu.roll(v, HD // 2, 1) * sine

    local(nk.at[:, columns], x_buf.at[0, xh, t], L_OWNK).wait()
    local(nv.at[:, columns], x_buf.at[1, xh, t], L_OWNV).wait()
    for n, (dx, dt) in enumerate(line):
        for kv, src in ((0, nk), (1, nv)):
            land = x_buf.at[kv, (xh - dx + 2) % 2, (t - dt + 4) % 4]
            remote(src.at[:, columns], land, LINE + 2 * n + kv, (g, t)).wait_recv()
    for kv, out in ((0, k_out), (1, v_out)):
        for i in (0, 1):
            out[i, z, y] = x_buf[kv, i].astype(F32).reshape(BLOCK, HD).astype(BF16)

    class Gather:
        def __init__(self, buf, first, second, at, base):
            self.buf, self.a, self.b, self.at, self.base = buf, first, second, at, base
            self.started = []

        def slot(self, da, db, half=None):
            p, q = (self.a + da + 4) % 4, (self.b + db + 4) % 4
            zz, yy = self.at(p, q)
            return self.buf.at[slice(None) if half is None else half, zz, yy]

        def dev(self, da, db):
            zz, yy = self.at((self.a + da + 4) % 4, (self.b + db + 4) % 4)
            return (group(xh, zz, yy), t)

        def send(self, src, i, da, db):
            c = remote(src, src, self.base + i, self.dev(da, db))
            c.start()
            self.started.append(c)

        def recv(self, land, i):
            remote(land, land, self.base + i, (g, t)).wait_recv()

        def first_own(self):
            self.send(self.slot(0, 0), 0, 1, 0)
            self.send(self.slot(0, 0), 1, -1, 0)

        def first_forward(self):
            self.recv(self.slot(-1, 0), 0)
            self.send(self.slot(-1, 0, 0), 2, 1, 0)
            self.recv(self.slot(1, 0), 1)
            self.send(self.slot(1, 0, 1), 3, -1, 0)

        def first_far(self):
            self.recv(self.slot(2, 0, 0), 2)
            self.recv(self.slot(2, 0, 1), 3)

        def second(self, s):
            self.send(self.slot(s, 0), 4 + 4 * (s % 4), 0, 1)
            self.send(self.slot(s, 0), 5 + 4 * (s % 4), 0, -1)

        def second_forward(self, s):
            i = 4 + 4 * (s % 4)
            self.recv(self.slot(s, -1), i)
            self.send(self.slot(s, -1, 0), i + 2, 0, 1)
            self.recv(self.slot(s, 1), i + 1)
            self.send(self.slot(s, 1, 1), i + 3, 0, -1)

        def second_far(self, s):
            i = 4 + 4 * (s % 4)
            self.recv(self.slot(s, 2, 0), i + 2)
            self.recv(self.slot(s, 2, 1), i + 3)

    keys = Gather(k_out, y, z, lambda p, q: (q, p), GATHER)
    values = Gather(v_out, z, y, lambda p, q: (p, q), GATHER + 20)
    both = (keys, values)
    for w in both:
        w.first_own()
    for w in both:
        w.second(0)

    local(hid, h_buf.at[t], L_HID).wait()
    for dt in (1, 2, 3):
        remote(hid, h_buf.at[(t - dt + 4) % 4], HIDDEN + dt - 1, (g, t)).wait_recv()
    squares = jnp.zeros((ROWS, HD), F32)
    for i in range(4):
        for j in range(WIDTH // HD):
            v = h_buf[i, :, j * HD : (j + 1) * HD].astype(F32)
            squares = squares + v * v
    inverse = lax.rsqrt(jnp.sum(squares, axis=1, keepdims=True) * (1.0 / D) + EPS)
    for i in range(CHUNKS):
        for j in range(CHUNK // HD):
            c = (i % 2) * (CHUNK // HD) + j
            v = h_buf[i // 2, :, c * HD : (c + 1) * HD].astype(F32)
            k = i * (CHUNK // HD) + j
            n_buf[i, :, j * HD : (j + 1) * HD] = (v * inverse * ig[k : k + 1, :]).astype(BF16)

    for w in both:
        w.first_forward()
    for w in both:
        w.second(-1)
    for w in both:
        w.second(1)

    def query_step(i, total):
        wq_copy(i).wait()
        return total + jnp.dot(n_buf[i], wq_s[i], preferred_element_type=F32)

    total = lax.fori_loop(0, CHUNKS // 2, query_step, jnp.zeros((ROWS, HEADS * HD), F32))
    for w in both:
        w.second_forward(0)
    for w in both:
        w.first_far()
    for w in both:
        w.second(2)
    total = lax.fori_loop(CHUNKS // 2, CHUNKS, query_step, total)

    q_s[...] = jnp.zeros_like(q_s)
    for h in range(HEADS):
        v = rotate(total[:, h * HD : (h + 1) * HD] + bq_s[h : h + 1, :])
        q_s[:, h, :] = v.astype(BF16).astype(F32)

    upper = lax.broadcasted_iota(jnp.int32, (16, 1), 0) < 8
    slot_ids = lax.broadcasted_iota(jnp.int32, (16, CACHE), 1)

    def attend(p, _):
        kc_copy(p).wait()
        vc_copy(p).wait()
        q2 = q_s[pl.ds(2 * p, 2)].reshape(16, HD)
        left = jnp.concatenate([jnp.where(upper, q2, 0.0), jnp.where(upper, 0.0, q2)], axis=1).astype(BF16)
        right = jnp.concatenate([kc_s[2 * p], kc_s[2 * p + 1]], axis=1)
        scores = lax.dot_general(left, right, (((1,), (1,)), ((), ())), preferred_element_type=F32) * SCALE
        length = jnp.where(upper, len_s[2 * p], len_s[2 * p + 1])
        scores = jnp.where(slot_ids < length, scores, -jnp.inf)
        peak = jnp.max(scores, axis=1, keepdims=True)
        weights = jnp.exp(scores - peak)
        total_weight = jnp.sum(weights, axis=1, keepdims=True)
        mixed = jnp.dot(
            weights.astype(BF16), jnp.concatenate([vc_s[2 * p], vc_s[2 * p + 1]], axis=1), preferred_element_type=F32
        )
        rows = pl.ds(2 * p, 2)
        o_s[rows] = jnp.where(upper, mixed[:, :HD], mixed[:, HD:]).reshape(2, 8, HD)
        m_s[rows] = jnp.broadcast_to(peak, (16, HD)).reshape(2, 8, HD)
        l_s[rows] = jnp.broadcast_to(total_weight, (16, HD)).reshape(2, 8, HD)
        return 0

    lax.fori_loop(0, 2, attend, 0)
    for w in both:
        w.second_forward(-1)
    lax.fori_loop(2, 4, attend, 0)
    for w in both:
        w.second_forward(1)
    lax.fori_loop(4, 6, attend, 0)
    for w in both:
        w.second_forward(2)
    lax.fori_loop(6, 8, attend, 0)
    for s in (0, -1, 1, 2):
        for w in both:
            w.second_far(s)

    def own_step(i, sums):
        x = n_buf[i]
        a, b = i // 4, i % 4
        return tuple(
            s + jnp.dot(x, out[a, b].reshape(CHUNK, HD), preferred_element_type=F32)
            for s, out in zip(sums, (k_out, v_out))
        )

    zero = jnp.zeros((ROWS, HD), F32)
    key_raw, value_raw = lax.fori_loop(0, CHUNKS, own_step, (zero, zero))
    new_key = rotate(key_raw + bk_s[...]).astype(BF16).astype(F32)
    new_value = (value_raw + bv_s[...]).astype(BF16).astype(F32)
    for h in range(HEADS):
        own_score = jnp.sum(q_s[:, h, :] * new_key, axis=1, keepdims=True) * SCALE
        peak = m_s[:, h, :]
        top = jnp.maximum(peak, own_score)
        a = jnp.exp(peak - top)
        b = jnp.exp(own_score - top)
        denominator = a * l_s[:, h, :] + b
        ctx_s[:, h * HD : (h + 1) * HD] = ((a * o_s[:, h, :] + b * new_value) / denominator).astype(BF16)

    for i in range(4):
        wo_copy(i).wait()
    share_copies = []
    for n, dt in enumerate((2, 1, 3)):
        to_t = (t + dt) % 4
        part = jnp.dot(ctx_s[...], wo_s[to_t], preferred_element_type=F32)
        send_buf[dt - 1] = part.astype(BF16)
        c = remote(send_buf.at[dt - 1], r_buf.at[dt - 1], SHARE + dt - 1, (g, to_t))
        c.start()
        share_copies.append(c)
    share = jnp.dot(ctx_s[...], wo_s[t], preferred_element_type=F32)
    for dt in (2, 1, 3):
        remote(send_buf.at[dt - 1], r_buf.at[dt - 1], SHARE + dt - 1, (g, t)).wait_recv()
    for i in range(3):
        share = share + r_buf[i].astype(F32)
    attended = share.astype(BF16)
    att_out[...] = attended
    residual = (h_buf[t].astype(F32) + attended.astype(F32)).astype(BF16).astype(F32)
    own_squares = jnp.sum(residual * residual, axis=1, keepdims=True)
    stat_send[...] = jnp.broadcast_to(own_squares, (ROWS, HD))
    stat_copies = []
    for dt in (1, 2, 3):
        c = remote(stat_send, stat_buf.at[dt - 1], STAT + dt - 1, (g, (t + dt) % 4))
        c.start()
        stat_copies.append(c)
    for dt in (1, 2, 3):
        remote(stat_send, stat_buf.at[dt - 1], STAT + dt - 1, (g, t)).wait_recv()
    square_total = own_squares + stat_buf[0] + stat_buf[1] + stat_buf[2]
    inverse_post = lax.rsqrt(square_total * (1.0 / D) + EPS)
    for j in range(WIDTH // HD):
        gain = pg[pl.ds(t * (WIDTH // HD) + j, 1), :]
        norm_out[:, j * HD : (j + 1) * HD] = (residual[:, j * HD : (j + 1) * HD] * inverse_post * gain).astype(BF16)

    for c in line_copies + hidden_copies + keys.started + values.started + share_copies + stat_copies:
        c.wait_send()


def shards(
    hidden_in, cache_lengths, in_gain, post_gain, w_query, b_query, b_key, b_value, w_out,
    key_cache, value_cache, next_key_weight, next_w_value,
):
    hbm = pl.BlockSpec(memory_space=pltpu.HBM)
    vmem = pl.BlockSpec(memory_space=pltpu.VMEM)
    attended, normed, key_out, value_out = pl.pallas_call(
        kernel,
        out_shape=[
            pltpu.VMEM((ROWS, WIDTH), BF16),
            pltpu.VMEM((ROWS, WIDTH), BF16),
            pltpu.VMEM((2, 4, 4, BLOCK, HD), BF16),
            pltpu.VMEM((2, 4, 4, BLOCK, HD), BF16),
        ],
        in_specs=[hbm] * 13,
        out_specs=[vmem] * 4,
        scratch_shapes=[
            pltpu.VMEM((4, ROWS, WIDTH), BF16),
            pltpu.SMEM((ROWS,), jnp.int32),
            pltpu.VMEM((D // HD, HD), F32),
            pltpu.VMEM((D // HD, HD), F32),
            pltpu.VMEM((HEADS, HD), F32),
            pltpu.VMEM((1, HD), F32),
            pltpu.VMEM((1, HD), F32),
            pltpu.VMEM((2, 2, 4, SHARD, HD), BF16),
            pltpu.VMEM((CHUNKS, CHUNK, HEADS * HD), BF16),
            pltpu.VMEM((ROWS, CACHE, HD), BF16),
            pltpu.VMEM((ROWS, CACHE, HD), BF16),
            pltpu.VMEM((4, HEADS * HD, WIDTH), BF16),
            pltpu.VMEM((CHUNKS, ROWS, CHUNK), BF16),
            pltpu.VMEM((ROWS, 8, HD), F32),
            pltpu.VMEM((ROWS, 8, HD), F32),
            pltpu.VMEM((ROWS, 8, HD), F32),
            pltpu.VMEM((ROWS, 8, HD), F32),
            pltpu.VMEM((ROWS, HEADS * HD), BF16),
            pltpu.VMEM((3, ROWS, WIDTH), BF16),
            pltpu.VMEM((3, ROWS, WIDTH), BF16),
            pltpu.VMEM((ROWS, HD), F32),
            pltpu.VMEM((3, ROWS, HD), F32),
            pltpu.SemaphoreType.DMA((LOCALS,)),
            pltpu.SemaphoreType.DMA((COPIES,)),
            pltpu.SemaphoreType.DMA((COPIES,)),
        ],
        compiler_params=pltpu.CompilerParams(
            collective_id=0, has_side_effects=True, vmem_limit_bytes=48 * 1024 * 1024
        ),
        name="decode",
    )(
        hidden_in,
        cache_lengths,
        in_gain.reshape(D // HD, HD),
        post_gain.reshape(D // HD, HD),
        w_query,
        b_query.reshape(HEADS, HD),
        b_key.reshape(1, HD),
        b_value.reshape(1, HD),
        w_out,
        key_cache.reshape(ROWS, CACHE, HD),
        value_cache.reshape(ROWS, CACHE, HD),
        next_key_weight,
        next_w_value,
    )
    return attended, normed, key_out.reshape(D, HD), value_out.reshape(D, HD)


def solution(mesh):
    in_specs = (
        P("grp", "tp"),
        P("grp"),
        P(),
        P(),
        P(None, "tp"),
        P("tp"),
        P("tp"),
        P("tp"),
        P("tp", None),
        P("grp", "tp", None, None),
        P("grp", "tp", None, None),
        P(("grp", "tp"), None),
        P(("grp", "tp"), None),
    )
    out_specs = (P("grp", "tp"), P("grp", "tp"), P(None, "tp"), P(None, "tp"))
    return jax.shard_map(shards, mesh=mesh, in_specs=in_specs, out_specs=out_specs, check_vma=False)
```

time: 454 us -> 51.2 us (0.11)
  waiting for transfers between devices: 403 us -> 0 us
  Pallas kernels: 0 us -> 40.2 us
  matrix products: 16.8 us -> 0 us
  between operations: 13.9 us -> 0.66 us
  blocking collectives: 12.1 us -> 0 us
  local copies, waits for them, and re-layouts: 3.64 us -> 9.78 us
    all_gather x2 -> x0, waiting for transfers between devices: 386 us -> none  [the longest x1 198 us: shards(): lax.all_gather(next_w_value, ('grp', 'tp'), axis=0, tiled=True)]
    pallas_call x0 -> x1, Pallas kernels: none -> 40.2 us  [shards(): pl.pallas_call(kernel, out_shape=[pltpu.VMEM((ROWS, WIDTH), BF16), pltpu....]
    dot_general x7 -> x0, matrix products: 16.8 us -> none  [the longest x1 4.49 us: shards(): partial_out = jnp.dot(context, w_out, preferred_element_type=jnp.float32)]
    reduce_scatter x1 -> x0, waiting for transfers between devices: 15.5 us -> none  [shards(): lax.psum_scatter(partial_out.astype(jnp.bfloat16), 'tp', scatter_dimensio...]
    unnamed x14 -> x22, local copies, waits for them, and re-layouts: 0.04 us -> 9.78 us
    all_gather x1 -> x0, blocking collectives: 6.97 us -> none  [shards(): full_rows = lax.all_gather(hidden_in, 'tp', axis=1, tiled=True)]
    psum x1 -> x0, blocking collectives: 5.17 us -> none  [shards(): square_total = lax.psum(jnp.sum(resid_f32 * resid_f32, axis=-1), 'tp')]
  transfers between devices with their start and end apart: 3 -> 0, of which waited for: 3 -> 0; matrix products, arithmetic and copies ran while one was open for 3% -> 0% of each run, Pallas kernels for 0% -> 0%
where the time goes in v1:
time: 51.2 us; the launch traced here: 50.7 us
  Pallas kernels  40.2 us (79%)
  local copies, waits for them, and re-layouts  9.78 us (19%)
  between operations  0.66 us (1%)
    pallas_call x1, Pallas kernels, shards(): pl.pallas_call(kernel, out_shape=[pltpu.VMEM((ROWS, WIDTH), BF16), pltpu....  40.2 us
    unnamed x22, local copies, waits for them, and re-layouts  9.78 us

profile of v1, /device:TPU:1, one launch (start us, length us, event | category | flops | bytes accessed | tf_op | source)
XLA Modules:
  0.0 50.7 jit_solution(11713006572126416212)
XLA Ops:
  0.6 0.0 copy-start
  0.6 0.8 %copy-done = bf16[16,1280]{1,0:T(8,128)(2,1)S(1)} copy-done((bf16[16,1280]{1,0:T(8,128)(2,1)S(1)}, bf16[16,1280]{1,0:T(8,128)(2,1)}, u32[]{:S(2)}) %copy-start) | copy-done | bytes 40984
  1.4 0.0 copy-start.1
  1.4 0.8 %copy-done.1 = bf16[40,512]{1,0:T(8,128)(2,1)S(1)} copy-done((bf16[40,512]{1,0:T(8,128)(2,1)S(1)}, bf16[40,512]{1,0:T(8,128)(2,1)}, u32[]{:S(2)}) %copy-start.1) | copy-done | bytes 40984
  2.2 0.0 copy-start.2
  2.2 0.8 %copy-done.2 = bf16[40,512]{1,0:T(8,128)(2,1)S(1)} copy-done((bf16[40,512]{1,0:T(8,128)(2,1)S(1)}, bf16[40,512]{1,0:T(8,128)(2,1)}, u32[]{:S(2)}) %copy-start.2) | copy-done | bytes 40984
  3.0 0.0 copy-start.3
  3.0 0.7 %copy-done.3 = f32[5120]{0:T(1024)S(1)} copy-done((f32[5120]{0:T(1024)S(1)}, f32[5120]{0:T(1024)}, u32[]{:S(2)}) %copy-start.3) | copy-done | bytes 20504
  3.7 0.0 copy-start.4
  3.7 0.7 %copy-done.4 = f32[5120]{0:T(1024)S(1)} copy-done((f32[5120]{0:T(1024)S(1)}, f32[5120]{0:T(1024)}, u32[]{:S(2)}) %copy-start.4) | copy-done | bytes 20504
  4.4 0.0 copy-start.5
  4.4 0.7 %copy-done.5 = f32[640]{0:T(1024)S(1)} copy-done((f32[640]{0:T(1024)S(1)}, f32[640]{0:T(1024)}, u32[]{:S(2)}) %copy-start.5) | copy-done | bytes 2584
  5.1 0.0 copy-start.6
  5.1 0.7 %copy-done.6 = s32[16]{0:T(128)S(1)} copy-done((s32[16]{0:T(128)S(1)}, s32[16]{0:T(128)}, u32[]{:S(2)}) %copy-start.6) | copy-done | bytes 88
  5.8 0.0 copy-start.7
  5.8 0.7 %copy-done.7 = f32[128]{0:T(128)S(1)} copy-done((f32[128]{0:T(128)S(1)}, f32[128]{0:T(128)}, u32[]{:S(2)}) %copy-start.7) | copy-done | bytes 536
  6.4 0.0 copy-start.8
  6.4 0.7 %copy-done.8 = f32[128]{0:T(128)S(1)} copy-done((f32[128]{0:T(128)S(1)}, f32[128]{0:T(128)}, u32[]{:S(2)}) %copy-start.8) | copy-done | bytes 536
  7.1 40.2 %decode.1 = (bf16[16,1280]{1,0:T(8,128)(2,1)S(1)}, bf16[16,1280]{1,0:T(8,128)(2,1)S(1)}, bf16[2,4,4,160,128]{4,3,2,1,0:T(8,128)(2,1)S(1)}, bf16[2,4,4,160,128]{4,3,2,1,0:T(8,128)(2,1)S(1)}) custom-call(bf16[16,1280]{1,0:T(8,128)(2,1)S(1)} %copy-done, s32[16]{0:T(128)S(1)} %copy-done.6, f32[40,128]{1,0:T(8,128)S(1)} %bitcast.11, f32[40,128]{1,0:T(8,128)S(1)} %bitcast.12, ...), custom_call_target="tpu_custom_call" | custom-call | tf_op jit(solution)/shard_map/decode/pallas_call | solution.py:357
  47.3 0.6 %copy.21 = bf16[16,1280]{1,0:T(8,128)(2,1)} copy(bf16[16,1280]{1,0:T(8,128)(2,1)S(1)} %get-tuple-element.12) | data formatting | bytes 81920
  48.0 0.6 %copy.22 = bf16[16,1280]{1,0:T(8,128)(2,1)} copy(bf16[16,1280]{1,0:T(8,128)(2,1)S(1)} %get-tuple-element.13) | data formatting | bytes 81920
  48.6 1.1 %copy.23 = bf16[5120,128]{1,0:T(8,128)(2,1)} copy(bf16[5120,128]{1,0:T(8,128)(2,1)S(1)} %bitcast.10) | data formatting | bytes 2621440
  49.6 1.1 %copy.24 = bf16[5120,128]{1,0:T(8,128)(2,1)} copy(bf16[5120,128]{1,0:T(8,128)(2,1)S(1)} %bitcast.9) | data formatting | bytes 2621440
Async XLA Ops:
  0.6 0.8 %copy-start = (bf16[16,1280]{1,0:T(8,128)(2,1)S(1)}, bf16[16,1280]{1,0:T(8,128)(2,1)}, u32[]{:S(2)}) copy-start(bf16[16,1280]{1,0:T(8,128)(2,1)} %hid.1) | copy-start | bytes 122884
  1.4 0.8 %copy-start.1 = (bf16[40,512]{1,0:T(8,128)(2,1)S(1)}, bf16[40,512]{1,0:T(8,128)(2,1)}, u32[]{:S(2)}) copy-start(bf16[40,512]{1,0:T(8,128)(2,1)} %nk.1) | copy-start | bytes 122884
  2.2 0.8 %copy-start.2 = (bf16[40,512]{1,0:T(8,128)(2,1)S(1)}, bf16[40,512]{1,0:T(8,128)(2,1)}, u32[]{:S(2)}) copy-start(bf16[40,512]{1,0:T(8,128)(2,1)} %nv.1) | copy-start | bytes 122884
  3.0 0.7 %copy-start.3 = (f32[5120]{0:T(1024)S(1)}, f32[5120]{0:T(1024)}, u32[]{:S(2)}) copy-start(f32[5120]{0:T(1024)} %param.15) | copy-start | bytes 61444
  3.7 0.7 %copy-start.4 = (f32[5120]{0:T(1024)S(1)}, f32[5120]{0:T(1024)}, u32[]{:S(2)}) copy-start(f32[5120]{0:T(1024)} %param.16) | copy-start | bytes 61444
  4.4 0.7 %copy-start.5 = (f32[640]{0:T(1024)S(1)}, f32[640]{0:T(1024)}, u32[]{:S(2)}) copy-start(f32[640]{0:T(1024)} %param.18) | copy-start | bytes 7684
  5.1 0.7 %copy-start.6 = (s32[16]{0:T(128)S(1)}, s32[16]{0:T(128)}, u32[]{:S(2)}) copy-start(s32[16]{0:T(128)} %lens.1) | copy-start | bytes 196
  5.8 0.7 %copy-start.7 = (f32[128]{0:T(128)S(1)}, f32[128]{0:T(128)}, u32[]{:S(2)}) copy-start(f32[128]{0:T(128)} %param.19) | copy-start | bytes 1540
  6.4 0.7 %copy-start.8 = (f32[128]{0:T(128)S(1)}, f32[128]{0:T(128)}, u32[]{:S(2)}) copy-start(f32[128]{0:T(128)} %param.20) | copy-start | bytes 1540

commit v2 on v1

--- a/solution.py
+++ b/solution.py
@@ -31,7 +31,9 @@
 GATHER = 17
 SHARE = 57
 STAT = 60
-COPIES = 63
+SLICE = 63
+PARTIAL = 69
+COPIES = 75
 L_HID, L_LEN, L_IN, L_POST, L_BQ, L_BK, L_BV, L_OWNK, L_OWNV = range(9)
 L_WQ = 9
 L_KC = L_WQ + CHUNKS
@@ -44,7 +46,8 @@
     hid, lens, in_gain, post_gain, wq, bq, bk, bv, wo, kc, vc, nk, nv,
     att_out, norm_out, k_out, v_out,
     h_buf, len_s, ig, pg, bq_s, bk_s, bv_s, x_buf, wq_s, kc_s, vc_s, wo_s,
-    n_buf, q_s, o_s, m_s, l_s, ctx_s, send_buf, r_buf, stat_send, stat_buf,
+    n_buf, n2_buf, nz_buf, ny_buf, pk_send, pv_send, pk_buf, pv_buf,
+    q_s, o_s, m_s, l_s, ctx_s, send_buf, r_buf, stat_send, stat_buf,
     lsem, ssem, rsem,
 ):
     g = lax.axis_index("grp")
@@ -80,8 +83,8 @@
     line = [(dx, dt) for dx in (0, 1) for dt in range(4) if (dx, dt) != (0, 0)]
     barrier = pltpu.get_barrier_semaphore()
     partners = [(group((xh + dx) % 2, z, y), (t + dt) % 4) for dx, dt in line]
-    partners += [(group(xh, z, (y + d) % 4), t) for d in (1, 3)]
-    partners += [(group(xh, (z + d) % 4, y), t) for d in (1, 3)]
+    partners += [(group(xh, z, (y + d) % 4), t) for d in (1, 2, 3)]
+    partners += [(group(xh, (z + d) % 4, y), t) for d in (1, 2, 3)]
     for dev in partners:
         pl.semaphore_signal(barrier, inc=1, device_id=dev, device_id_type=MESH)
 
@@ -99,6 +102,14 @@
 
     pl.semaphore_wait(barrier, len(partners))
 
+    far_t, twin_t = (t + 2) % 4, t + 1 - 2 * (t % 2)
+    far_twin = (twin_t + 2) % 4
+    hidden_copies = [
+        remote(hid, h_buf.at[t], HIDDEN, (g, far_t)),
+        remote(hid, h_buf.at[t], HIDDEN + 1, (g, twin_t)),
+    ]
+    for c in hidden_copies:
+        c.start()
     line_copies = []
     for n, (dx, dt) in enumerate(line):
         to_t = (t + dt) % 4
@@ -108,12 +119,6 @@
             c = remote(src.at[:, cols], x_buf.at[kv, xh, t], LINE + 2 * n + kv, dev)
             c.start()
             line_copies.append(c)
-    hidden_copies = []
-    for dt in (1, 2, 3):
-        c = remote(hid, h_buf.at[t], HIDDEN + dt - 1, (g, (t + dt) % 4))
-        c.start()
-        hidden_copies.append(c)
-
     def start_all(make, count):
         def body(i, _):
             make(i).start()
@@ -141,79 +146,13 @@
     def rotate(v):
         return v * cosine + pltpu.roll(v, HD // 2, 1) * sine
 
-    local(nk.at[:, columns], x_buf.at[0, xh, t], L_OWNK).wait()
-    local(nv.at[:, columns], x_buf.at[1, xh, t], L_OWNV).wait()
-    for n, (dx, dt) in enumerate(line):
-        for kv, src in ((0, nk), (1, nv)):
-            land = x_buf.at[kv, (xh - dx + 2) % 2, (t - dt + 4) % 4]
-            remote(src.at[:, columns], land, LINE + 2 * n + kv, (g, t)).wait_recv()
-    for kv, out in ((0, k_out), (1, v_out)):
-        for i in (0, 1):
-            out[i, z, y] = x_buf[kv, i].astype(F32).reshape(BLOCK, HD).astype(BF16)
-
-    class Gather:
-        def __init__(self, buf, first, second, at, base):
-            self.buf, self.a, self.b, self.at, self.base = buf, first, second, at, base
-            self.started = []
-
-        def slot(self, da, db, half=None):
-            p, q = (self.a + da + 4) % 4, (self.b + db + 4) % 4
-            zz, yy = self.at(p, q)
-            return self.buf.at[slice(None) if half is None else half, zz, yy]
-
-        def dev(self, da, db):
-            zz, yy = self.at((self.a + da + 4) % 4, (self.b + db + 4) % 4)
-            return (group(xh, zz, yy), t)
-
-        def send(self, src, i, da, db):
-            c = remote(src, src, self.base + i, self.dev(da, db))
-            c.start()
-            self.started.append(c)
-
-        def recv(self, land, i):
-            remote(land, land, self.base + i, (g, t)).wait_recv()
-
-        def first_own(self):
-            self.send(self.slot(0, 0), 0, 1, 0)
-            self.send(self.slot(0, 0), 1, -1, 0)
-
-        def first_forward(self):
-            self.recv(self.slot(-1, 0), 0)
-            self.send(self.slot(-1, 0, 0), 2, 1, 0)
-            self.recv(self.slot(1, 0), 1)
-            self.send(self.slot(1, 0, 1), 3, -1, 0)
-
-        def first_far(self):
-            self.recv(self.slot(2, 0, 0), 2)
-            self.recv(self.slot(2, 0, 1), 3)
-
-        def second(self, s):
-            self.send(self.slot(s, 0), 4 + 4 * (s % 4), 0, 1)
-            self.send(self.slot(s, 0), 5 + 4 * (s % 4), 0, -1)
-
-        def second_forward(self, s):
-            i = 4 + 4 * (s % 4)
-            self.recv(self.slot(s, -1), i)
-            self.send(self.slot(s, -1, 0), i + 2, 0, 1)
-            self.recv(self.slot(s, 1), i + 1)
-            self.send(self.slot(s, 1, 1), i + 3, 0, -1)
-
-        def second_far(self, s):
-            i = 4 + 4 * (s % 4)
-            self.recv(self.slot(s, 2, 0), i + 2)
-            self.recv(self.slot(s, 2, 1), i + 3)
-
-    keys = Gather(k_out, y, z, lambda p, q: (q, p), GATHER)
-    values = Gather(v_out, z, y, lambda p, q: (p, q), GATHER + 20)
-    both = (keys, values)
-    for w in both:
-        w.first_own()
-    for w in both:
-        w.second(0)
-
     local(hid, h_buf.at[t], L_HID).wait()
-    for dt in (1, 2, 3):
-        remote(hid, h_buf.at[(t - dt + 4) % 4], HIDDEN + dt - 1, (g, t)).wait_recv()
+    remote(hid, h_buf.at[far_t], HIDDEN, (g, t)).wait_recv()
+    relay = remote(h_buf.at[far_t], h_buf.at[far_t], HIDDEN + 2, (g, twin_t))
+    relay.start()
+    hidden_copies.append(relay)
+    remote(hid, h_buf.at[twin_t], HIDDEN + 1, (g, t)).wait_recv()
+    remote(hid, h_buf.at[far_twin], HIDDEN + 2, (g, t)).wait_recv()
     squares = jnp.zeros((ROWS, HD), F32)
     for i in range(4):
         for j in range(WIDTH // HD):
@@ -225,39 +164,104 @@
             c = (i % 2) * (CHUNK // HD) + j
             v = h_buf[i // 2, :, c * HD : (c + 1) * HD].astype(F32)
             k = i * (CHUNK // HD) + j
-            n_buf[i, :, j * HD : (j + 1) * HD] = (v * inverse * ig[k : k + 1, :]).astype(BF16)
-
-    for w in both:
-        w.first_forward()
-    for w in both:
-        w.second(-1)
-    for w in both:
-        w.second(1)
-
-    def query_step(i, total):
+            n_buf[i // 4, i % 4, :, j * HD : (j + 1) * HD] = (v * inverse * ig[k : k + 1, :]).astype(BF16)
+
+    for b in range(4):
+        n2_buf[b] = jnp.concatenate(
+            [n_buf[i // 4, i % 4, :, b * BLOCK : (b + 1) * BLOCK].astype(F32) for i in range(CHUNKS)], axis=1
+        ).astype(BF16)
+    nz_buf[z] = n_buf[:, z]
+    ny_buf[y] = n2_buf[y]
+    slice_copies = []
+    for d in (1, 2, 3):
+        zz, yy = (z + d) % 4, (y + d) % 4
+        slice_copies.append(remote(n_buf.at[:, zz], nz_buf.at[z], SLICE + d - 1, (group(xh, zz, y), t)))
+        slice_copies.append(remote(n2_buf.at[yy], ny_buf.at[y], SLICE + d + 2, (group(xh, z, yy), t)))
+    for c in slice_copies:
+        c.start()
+
+    local(nk.at[:, columns], x_buf.at[0, xh, t], L_OWNK).wait()
+    local(nv.at[:, columns], x_buf.at[1, xh, t], L_OWNV).wait()
+    for n, (dx, dt) in enumerate(line):
+        for kv, src in ((0, nk), (1, nv)):
+            land = x_buf.at[kv, (xh - dx + 2) % 2, (t - dt + 4) % 4]
+            remote(src.at[:, columns], land, LINE + 2 * n + kv, (g, t)).wait_recv()
+    for kv, out in ((0, k_out), (1, v_out)):
+        for i in (0, 1):
+            out[i, z, y] = x_buf[kv, i].astype(F32).reshape(BLOCK, HD).astype(BF16)
+
+    class Gather:
+        def __init__(self, buf, first, second, at, base):
+            self.buf, self.a, self.b, self.at, self.base = buf, first, second, at, base
+            self.started = []
+
+        def slot(self, da, db, half=None):
+            p, q = (self.a + da + 4) % 4, (self.b + db + 4) % 4
+            zz, yy = self.at(p, q)
+            return self.buf.at[slice(None) if half is None else half, zz, yy]
+
+        def dev(self, da, db):
+            zz, yy = self.at((self.a + da + 4) % 4, (self.b + db + 4) % 4)
+            return (group(xh, zz, yy), t)
+
+        def send(self, src, i, da, db):
+            c = remote(src, src, self.base + i, self.dev(da, db))
+            c.start()
+            self.started.append(c)
+
+        def recv(self, land, i):
+            remote(land, land, self.base + i, (g, t)).wait_recv()
+
+        def first_own(self):
+            for i, d in enumerate((1, -1, 2)):
+                self.send(self.slot(0, 0), i, d, 0)
+
+        def first_near(self):
+            self.recv(self.slot(-1, 0), 0)
+            self.recv(self.slot(1, 0), 1)
+
+        def first_far(self):
+            self.recv(self.slot(2, 0), 2)
+
+        def second(self, s):
+            self.send(self.slot(s, 0), 4 + 4 * (s % 4), 0, 1)
+            self.send(self.slot(s, 0), 5 + 4 * (s % 4), 0, -1)
+
+        def second_forward(self, s):
+            i = 4 + 4 * (s % 4)
+            self.recv(self.slot(s, -1), i)
+            self.send(self.slot(s, -1, 0), i + 2, 0, 1)
+            self.recv(self.slot(s, 1), i + 1)
+            self.send(self.slot(s, 1, 1), i + 3, 0, -1)
+
+        def second_far(self, s):
+            i = 4 + 4 * (s % 4)
+            self.recv(self.slot(s, 2, 0), i + 2)
+            self.recv(self.slot(s, 2, 1), i + 3)
+
+    keys = Gather(k_out, y, z, lambda p, q: (q, p), GATHER)
+    values = Gather(v_out, z, y, lambda p, q: (p, q), GATHER + 20)
+    both = (keys, values)
+    for w in both:
+        w.first_own()
+
+    for i in range(CHUNKS):
         wq_copy(i).wait()
-        return total + jnp.dot(n_buf[i], wq_s[i], preferred_element_type=F32)
-
-    total = lax.fori_loop(0, CHUNKS // 2, query_step, jnp.zeros((ROWS, HEADS * HD), F32))
-    for w in both:
-        w.second_forward(0)
-    for w in both:
-        w.first_far()
-    for w in both:
-        w.second(2)
-    total = lax.fori_loop(CHUNKS // 2, CHUNKS, query_step, total)
-
+    total = jnp.dot(n_buf[0, 0], wq_s[0], preferred_element_type=F32)
+    for i in range(1, CHUNKS):
+        total = total + jnp.dot(n_buf[i // 4, i % 4], wq_s[i], preferred_element_type=F32)
     q_s[...] = jnp.zeros_like(q_s)
     for h in range(HEADS):
         v = rotate(total[:, h * HD : (h + 1) * HD] + bq_s[h : h + 1, :])
         q_s[:, h, :] = v.astype(BF16).astype(F32)
 
+    for w in both:
+        w.second(0)
+
     upper = lax.broadcasted_iota(jnp.int32, (16, 1), 0) < 8
     slot_ids = lax.broadcasted_iota(jnp.int32, (16, CACHE), 1)
 
-    def attend(p, _):
-        kc_copy(p).wait()
-        vc_copy(p).wait()
+    def attend(p):
         q2 = q_s[pl.ds(2 * p, 2)].reshape(16, HD)
         left = jnp.concatenate([jnp.where(upper, q2, 0.0), jnp.where(upper, 0.0, q2)], axis=1).astype(BF16)
         right = jnp.concatenate([kc_s[2 * p], kc_s[2 * p + 1]], axis=1)
@@ -274,32 +278,57 @@
         o_s[rows] = jnp.where(upper, mixed[:, :HD], mixed[:, HD:]).reshape(2, 8, HD)
         m_s[rows] = jnp.broadcast_to(peak, (16, HD)).reshape(2, 8, HD)
         l_s[rows] = jnp.broadcast_to(total_weight, (16, HD)).reshape(2, 8, HD)
+
+    def attend_twice(i, _):
+        for p in (2 * i, 2 * i + 1):
+            kc_copy(p).wait()
+            vc_copy(p).wait()
+        for p in (2 * i, 2 * i + 1):
+            attend(p)
         return 0
 
-    lax.fori_loop(0, 2, attend, 0)
-    for w in both:
-        w.second_forward(-1)
-    lax.fori_loop(2, 4, attend, 0)
-    for w in both:
-        w.second_forward(1)
-    lax.fori_loop(4, 6, attend, 0)
-    for w in both:
-        w.second_forward(2)
-    lax.fori_loop(6, 8, attend, 0)
-    for s in (0, -1, 1, 2):
-        for w in both:
-            w.second_far(s)
-
-    def own_step(i, sums):
-        x = n_buf[i]
-        a, b = i // 4, i % 4
-        return tuple(
-            s + jnp.dot(x, out[a, b].reshape(CHUNK, HD), preferred_element_type=F32)
-            for s, out in zip(sums, (k_out, v_out))
+    lax.fori_loop(0, 3, attend_twice, 0)
+    for w in both:
+        w.first_near()
+    for w in both:
+        w.second(-1)
+    for w in both:
+        w.second(1)
+
+    for w in both:
+        w.first_far()
+    for d in (1, 2, 3):
+        zz, yy = (z - d + 4) % 4, (y - d + 4) % 4
+        remote(n_buf.at[:, z], nz_buf.at[zz], SLICE + d - 1, (g, t)).wait_recv()
+        remote(n2_buf.at[y], ny_buf.at[yy], SLICE + d + 2, (g, t)).wait_recv()
+    key_part = jnp.zeros((4 * ROWS, HD), F32)
+    for i in (0, 1):
+        key_part = key_part + jnp.dot(
+            nz_buf[:, i].reshape(4 * ROWS, CHUNK), k_out[i, z].reshape(CHUNK, HD), preferred_element_type=F32
         )
-
-    zero = jnp.zeros((ROWS, HD), F32)
-    key_raw, value_raw = lax.fori_loop(0, CHUNKS, own_step, (zero, zero))
+    pk_send[...] = key_part.reshape(4, ROWS, HD)
+    value_part = jnp.dot(
+        ny_buf[...].reshape(4 * ROWS, 2 * CHUNK), v_out[:, :, y].reshape(2 * CHUNK, HD), preferred_element_type=F32
+    )
+    pv_send[...] = value_part.reshape(4, ROWS, HD)
+    partial_copies = []
+    for d in (1, 2, 3):
+        zz, yy = (z + d) % 4, (y + d) % 4
+        partial_copies.append(remote(pk_send.at[zz], pk_buf.at[d - 1], PARTIAL + d - 1, (group(xh, zz, y), t)))
+        partial_copies.append(remote(pv_send.at[yy], pv_buf.at[d - 1], PARTIAL + d + 2, (group(xh, z, yy), t)))
+    for c in partial_copies:
+        c.start()
+    for w in both:
+        w.second(2)
+    attend_twice(3, 0)
+    for w in both:
+        w.second_forward(0)
+
+    for d in (1, 2, 3):
+        remote(pk_send.at[z], pk_buf.at[d - 1], PARTIAL + d - 1, (g, t)).wait_recv()
+        remote(pv_send.at[y], pv_buf.at[d - 1], PARTIAL + d + 2, (g, t)).wait_recv()
+    key_raw = pk_send[z] + pk_buf[0] + pk_buf[1] + pk_buf[2]
+    value_raw = pv_send[y] + pv_buf[0] + pv_buf[1] + pv_buf[2]
     new_key = rotate(key_raw + bk_s[...]).astype(BF16).astype(F32)
     new_value = (value_raw + bv_s[...]).astype(BF16).astype(F32)
     for h in range(HEADS):
@@ -322,6 +351,12 @@
         c.start()
         share_copies.append(c)
     share = jnp.dot(ctx_s[...], wo_s[t], preferred_element_type=F32)
+    for w in both:
+        w.second_forward(-1)
+    for w in both:
+        w.second_forward(1)
+    for w in both:
+        w.second_forward(2)
     for dt in (2, 1, 3):
         remote(send_buf.at[dt - 1], r_buf.at[dt - 1], SHARE + dt - 1, (g, t)).wait_recv()
     for i in range(3):
@@ -336,6 +371,12 @@
         c = remote(stat_send, stat_buf.at[dt - 1], STAT + dt - 1, (g, (t + dt) % 4))
         c.start()
         stat_copies.append(c)
+    for w in both:
+        w.second_far(0)
+    for w in both:
+        w.second_far(-1)
+    for w in both:
+        w.second_far(1)
     for dt in (1, 2, 3):
         remote(stat_send, stat_buf.at[dt - 1], STAT + dt - 1, (g, t)).wait_recv()
     square_total = own_squares + stat_buf[0] + stat_buf[1] + stat_buf[2]
@@ -344,8 +385,19 @@
         gain = pg[pl.ds(t * (WIDTH // HD) + j, 1), :]
         norm_out[:, j * HD : (j + 1) * HD] = (residual[:, j * HD : (j + 1) * HD] * inverse_post * gain).astype(BF16)
 
-    for c in line_copies + hidden_copies + keys.started + values.started + share_copies + stat_copies:
+    for w in both:
+        w.second_far(2)
+    for c in line_copies + hidden_copies + slice_copies + partial_copies + keys.started + values.started + share_copies + stat_copies:
         c.wait_send()
+
+
+def store(*refs):
+    sources, targets, sems = refs[:4], refs[4:8], refs[8]
+    copies = [pltpu.make_async_copy(a, b, sems.at[i]) for i, (a, b) in enumerate(zip(sources, targets))]
+    for c in copies:
+        c.start()
+    for c in copies:
+        c.wait()
 
 
 def shards(
@@ -354,6 +406,21 @@
 ):
     hbm = pl.BlockSpec(memory_space=pltpu.HBM)
     vmem = pl.BlockSpec(memory_space=pltpu.VMEM)
+    operands = (
+        hidden_in,
+        cache_lengths,
+        in_gain.reshape(D // HD, HD),
+        post_gain.reshape(D // HD, HD),
+        w_query,
+        b_query.reshape(HEADS, HD),
+        b_key.reshape(1, HD),
+        b_value.reshape(1, HD),
+        w_out,
+        key_cache.reshape(ROWS, CACHE, HD),
+        value_cache.reshape(ROWS, CACHE, HD),
+        next_key_weight,
+        next_w_value,
+    )
     attended, normed, key_out, value_out = pl.pallas_call(
         kernel,
         out_shape=[
@@ -377,7 +444,14 @@
             pltpu.VMEM((ROWS, CACHE, HD), BF16),
             pltpu.VMEM((ROWS, CACHE, HD), BF16),
             pltpu.VMEM((4, HEADS * HD, WIDTH), BF16),
-            pltpu.VMEM((CHUNKS, ROWS, CHUNK), BF16),
+            pltpu.VMEM((2, 4, ROWS, CHUNK), BF16),
+            pltpu.VMEM((4, ROWS, 2 * CHUNK), BF16),
+            pltpu.VMEM((4, 2, ROWS, CHUNK), BF16),
+            pltpu.VMEM((4, ROWS, 2 * CHUNK), BF16),
+            pltpu.VMEM((4, ROWS, HD), F32),
+            pltpu.VMEM((4, ROWS, HD), F32),
+            pltpu.VMEM((3, ROWS, HD), F32),
+            pltpu.VMEM((3, ROWS, HD), F32),
             pltpu.VMEM((ROWS, 8, HD), F32),
             pltpu.VMEM((ROWS, 8, HD), F32),
             pltpu.VMEM((ROWS, 8, HD), F32),
@@ -395,22 +469,16 @@
             collective_id=0, has_side_effects=True, vmem_limit_bytes=48 * 1024 * 1024
         ),
         name="decode",
-    )(
-        hidden_in,
-        cache_lengths,
-        in_gain.reshape(D // HD, HD),
-        post_gain.reshape(D // HD, HD),
-        w_query,
-        b_query.reshape(HEADS, HD),
-        b_key.reshape(1, HD),
-        b_value.reshape(1, HD),
-        w_out,
-        key_cache.reshape(ROWS, CACHE, HD),
-        value_cache.reshape(ROWS, CACHE, HD),
-        next_key_weight,
-        next_w_value,
-    )
-    return attended, normed, key_out.reshape(D, HD), value_out.reshape(D, HD)
+    )(*[pltpu.with_memory_space_constraint(a, pltpu.HBM) for a in operands])
+    results = (attended, normed, key_out.reshape(D, HD), value_out.reshape(D, HD))
+    return pl.pallas_call(
+        store,
+        out_shape=[jax.ShapeDtypeStruct(a.shape, a.dtype) for a in results],
+        in_specs=[pl.BlockSpec(memory_space=pltpu.VMEM)] * 4,
+        out_specs=[hbm] * 4,
+        scratch_shapes=[pltpu.SemaphoreType.DMA((4,))],
+        name="store",
+    )(*[pltpu.with_memory_space_constraint(a, pltpu.VMEM) for a in results])
 
 
 def solution(mesh):

time: 51.2 us -> 37.7 us (0.74)
  local copies, waits for them, and re-layouts: 9.78 us -> 0 us
  Pallas kernels: 40.2 us -> 36.9 us
    unnamed x22 -> x0, local copies, waits for them, and re-layouts: 9.78 us -> none
    pallas_call x1, Pallas kernels: 40.2 us -> 35.4 us  [shards(): pl.pallas_call(kernel, out_shape=[pltpu.VMEM((ROWS, WIDTH), BF16), pltpu....]
    pallas_call x0 -> x1, Pallas kernels: none -> 1.55 us  [shards(): pl.pallas_call(store, out_shape=[jax.ShapeDtypeStruct(a.shape, a.dtype) f...]
where the time goes in v2:
time: 37.7 us; the launch traced here: 37.6 us
  Pallas kernels  36.9 us (98%)
  between operations  0.64 us (2%)
    pallas_call x1, Pallas kernels, shards(): pl.pallas_call(kernel, out_shape=[pltpu.VMEM((ROWS, WIDTH), BF16), pltpu....  35.4 us
    pallas_call x1, Pallas kernels, shards(): pl.pallas_call(store, out_shape=[jax.ShapeDtypeStruct(a.shape, a.dtype) f...  1.55 us

profile of v2, /device:TPU:1, one launch (start us, length us, event | category | flops | bytes accessed | tf_op | source)
XLA Modules:
  0.0 37.6 jit_solution(10414499937925217063)
XLA Ops:
  0.6 35.4 %decode.1 = (bf16[16,1280]{1,0:T(8,128)(2,1)S(1)}, bf16[16,1280]{1,0:T(8,128)(2,1)S(1)}, bf16[2,4,4,160,128]{4,3,2,1,0:T(8,128)(2,1)S(1)}, bf16[2,4,4,160,128]{4,3,2,1,0:T(8,128)(2,1)S(1)}) custom-call(bf16[16,1280]{1,0:T(8,128)(2,1)} %hid.1, s32[16]{0:T(128)} %lens.1, f32[40,128]{1,0:T(8,128)} %bitcast.13, f32[40,128]{1,0:T(8,128)} %bitcast.14, ...), custom_call_target="tpu_custom_call" | custom-call | tf_op jit(solution)/shard_map/decode/pallas_call | solution.py:424
  36.0 1.6 %store.1 = (bf16[16,1280]{1,0:T(8,128)(2,1)}, bf16[16,1280]{1,0:T(8,128)(2,1)}, bf16[5120,128]{1,0:T(8,128)(2,1)}, bf16[5120,128]{1,0:T(8,128)(2,1)}) custom-call(bf16[16,1280]{1,0:T(8,128)(2,1)S(1)} %get-tuple-element.8.refs_0_, bf16[16,1280]{1,0:T(8,128)(2,1)S(1)} %get-tuple-element.9.refs_1_, bf16[5120,128]{1,0:T(8,128)(2,1)S(1)} %bitcast.9, ...), custom_call_target="tpu_custom_call" | custom-call | tf_op jit(solution)/shard_map/store/pallas_call | solution.py:474

commit v3 on v2

--- a/solution.py
+++ b/solution.py
@@ -29,11 +29,12 @@
 HIDDEN = 0
 LINE = 3
 GATHER = 17
-SHARE = 57
-STAT = 60
-SLICE = 63
-PARTIAL = 69
-COPIES = 75
+SHARE = 63
+STAT = 67
+SLICE = 69
+TWIN = 75
+PARTIAL = 81
+COPIES = 87
 L_HID, L_LEN, L_IN, L_POST, L_BQ, L_BK, L_BV, L_OWNK, L_OWNV = range(9)
 L_WQ = 9
 L_KC = L_WQ + CHUNKS
@@ -80,7 +81,7 @@
     for c in small:
         c.start()
 
-    line = [(dx, dt) for dx in (0, 1) for dt in range(4) if (dx, dt) != (0, 0)]
+    line = [(dx, dt) for dx in (1, 0) for dt in range(4) if (dx, dt) != (0, 0)]
     barrier = pltpu.get_barrier_semaphore()
     partners = [(group((xh + dx) % 2, z, y), (t + dt) % 4) for dx, dt in line]
     partners += [(group(xh, z, (y + d) % 4), t) for d in (1, 2, 3)]
@@ -167,16 +168,22 @@
             n_buf[i // 4, i % 4, :, j * HD : (j + 1) * HD] = (v * inverse * ig[k : k + 1, :]).astype(BF16)
 
     for b in range(4):
-        n2_buf[b] = jnp.concatenate(
-            [n_buf[i // 4, i % 4, :, b * BLOCK : (b + 1) * BLOCK].astype(F32) for i in range(CHUNKS)], axis=1
-        ).astype(BF16)
+        for a in (0, 1):
+            n2_buf[b, a] = jnp.concatenate(
+                [n_buf[a, i, :, b * BLOCK : (b + 1) * BLOCK].astype(F32) for i in range(4)], axis=1
+            ).astype(BF16)
     nz_buf[z] = n_buf[:, z]
     ny_buf[y] = n2_buf[y]
+    core = t % 2
     slice_copies = []
     for d in (1, 2, 3):
         zz, yy = (z + d) % 4, (y + d) % 4
-        slice_copies.append(remote(n_buf.at[:, zz], nz_buf.at[z], SLICE + d - 1, (group(xh, zz, y), t)))
-        slice_copies.append(remote(n2_buf.at[yy], ny_buf.at[y], SLICE + d + 2, (group(xh, z, yy), t)))
+        slice_copies.append(
+            remote(n_buf.at[core, zz], nz_buf.at[z, core], SLICE + d - 1, (group(xh, zz, y), t))
+        )
+        slice_copies.append(
+            remote(n2_buf.at[yy, core], ny_buf.at[y, core], SLICE + d + 2, (group(xh, z, yy), t))
+        )
     for c in slice_copies:
         c.start()
 
@@ -224,23 +231,53 @@
             self.recv(self.slot(2, 0), 2)
 
         def second(self, s):
-            self.send(self.slot(s, 0), 4 + 4 * (s % 4), 0, 1)
-            self.send(self.slot(s, 0), 5 + 4 * (s % 4), 0, -1)
+            half = xh if s == 0 else None
+            self.send(self.slot(s, 0, half), 4 + 4 * (s % 4), 0, 1)
+            self.send(self.slot(s, 0, half), 5 + 4 * (s % 4), 0, -1)
+            if s == 2:
+                self.send(self.slot(2, 0), 14, 0, 2)
+
+        def piece(self, s, db, part):
+            if s == 0:
+                return self.slot(0, db, xh).at[pl.ds(part * (BLOCK // 2), BLOCK // 2)]
+            return self.slot(s, db, part)
 
         def second_forward(self, s):
             i = 4 + 4 * (s % 4)
-            self.recv(self.slot(s, -1), i)
-            self.send(self.slot(s, -1, 0), i + 2, 0, 1)
-            self.recv(self.slot(s, 1), i + 1)
-            self.send(self.slot(s, 1, 1), i + 3, 0, -1)
+            half = xh if s == 0 else None
+            self.recv(self.slot(s, -1, half), i)
+            self.send(self.piece(s, -1, 0), i + 2, 0, 1)
+            self.recv(self.slot(s, 1, half), i + 1)
+            self.send(self.piece(s, 1, 1), i + 3, 0, -1)
 
         def second_far(self, s):
             i = 4 + 4 * (s % 4)
-            self.recv(self.slot(s, 2, 0), i + 2)
-            self.recv(self.slot(s, 2, 1), i + 3)
+            if s == 2:
+                for k, db in enumerate((-1, 1, 2)):
+                    self.recv(self.slot(2, db), i + k)
+                return
+            self.recv(self.piece(s, 2, 0), i + 2)
+            self.recv(self.piece(s, 2, 1), i + 3)
+
+        def cross(self, i, db):
+            half = self.slot(0, db, xh)
+            c = remote(half, half, self.base + 20 + i, (group(1 - xh, z, y), t))
+            c.start()
+            self.started.append(c)
+
+        def cross_near(self):
+            self.cross(0, -1)
+            self.cross(1, 1)
+
+        def cross_far(self):
+            self.cross(2, 2)
+
+        def crossed(self):
+            for i, db in enumerate((-1, 1, 2)):
+                self.recv(self.slot(0, db, 1 - xh), 20 + i)
 
     keys = Gather(k_out, y, z, lambda p, q: (q, p), GATHER)
-    values = Gather(v_out, z, y, lambda p, q: (p, q), GATHER + 20)
+    values = Gather(v_out, z, y, lambda p, q: (p, q), GATHER + 23)
     both = (keys, values)
     for w in both:
         w.first_own()
@@ -287,29 +324,39 @@
             attend(p)
         return 0
 
-    lax.fori_loop(0, 3, attend_twice, 0)
+    lax.fori_loop(0, 2, attend_twice, 0)
+    twin_copies = []
+    for d in (1, 2, 3):
+        zz, yy = (z - d + 4) % 4, (y - d + 4) % 4
+        for land, i in ((nz_buf.at[zz, core], d - 1), (ny_buf.at[yy, core], d + 2)):
+            remote(land, land, SLICE + i, (g, t)).wait_recv()
+            c = remote(land, land, TWIN + i, (g, twin_t))
+            c.start()
+            twin_copies.append(c)
     for w in both:
         w.first_near()
     for w in both:
         w.second(-1)
-    for w in both:
-        w.second(1)
-
+    attend_twice(2, 0)
     for w in both:
         w.first_far()
     for d in (1, 2, 3):
         zz, yy = (z - d + 4) % 4, (y - d + 4) % 4
-        remote(n_buf.at[:, z], nz_buf.at[zz], SLICE + d - 1, (g, t)).wait_recv()
-        remote(n2_buf.at[y], ny_buf.at[yy], SLICE + d + 2, (g, t)).wait_recv()
+        theirs = nz_buf.at[zz, 1 - core]
+        remote(theirs, theirs, TWIN + d - 1, (g, t)).wait_recv()
+        theirs = ny_buf.at[yy, 1 - core]
+        remote(theirs, theirs, TWIN + d + 2, (g, t)).wait_recv()
     key_part = jnp.zeros((4 * ROWS, HD), F32)
     for i in (0, 1):
         key_part = key_part + jnp.dot(
             nz_buf[:, i].reshape(4 * ROWS, CHUNK), k_out[i, z].reshape(CHUNK, HD), preferred_element_type=F32
         )
     pk_send[...] = key_part.reshape(4, ROWS, HD)
-    value_part = jnp.dot(
-        ny_buf[...].reshape(4 * ROWS, 2 * CHUNK), v_out[:, :, y].reshape(2 * CHUNK, HD), preferred_element_type=F32
-    )
+    value_part = jnp.zeros((4 * ROWS, HD), F32)
+    for i in (0, 1):
+        value_part = value_part + jnp.dot(
+            ny_buf[:, i].reshape(4 * ROWS, CHUNK), v_out[i, :, y].reshape(CHUNK, HD), preferred_element_type=F32
+        )
     pv_send[...] = value_part.reshape(4, ROWS, HD)
     partial_copies = []
     for d in (1, 2, 3):
@@ -319,10 +366,21 @@
     for c in partial_copies:
         c.start()
     for w in both:
+        w.second_forward(0)
+    for w in both:
+        w.cross_near()
+    for w in both:
+        w.second(1)
+    for w in both:
         w.second(2)
     attend_twice(3, 0)
-    for w in both:
-        w.second_forward(0)
+
+    for w in both:
+        w.second_far(0)
+    for w in both:
+        w.cross_far()
+    for w in both:
+        w.second_forward(-1)
 
     for d in (1, 2, 3):
         remote(pk_send.at[z], pk_buf.at[d - 1], PARTIAL + d - 1, (g, t)).wait_recv()
@@ -343,43 +401,48 @@
     for i in range(4):
         wo_copy(i).wait()
     share_copies = []
-    for n, dt in enumerate((2, 1, 3)):
-        to_t = (t + dt) % 4
-        part = jnp.dot(ctx_s[...], wo_s[to_t], preferred_element_type=F32)
-        send_buf[dt - 1] = part.astype(BF16)
-        c = remote(send_buf.at[dt - 1], r_buf.at[dt - 1], SHARE + dt - 1, (g, to_t))
+    share_copies = []
+
+    def share(n, value, to_t):
+        send_buf[n] = value.astype(BF16)
+        c = remote(send_buf.at[n], r_buf.at[n], SHARE + n, (g, to_t))
         c.start()
         share_copies.append(c)
-    share = jnp.dot(ctx_s[...], wo_s[t], preferred_element_type=F32)
-    for w in both:
-        w.second_forward(-1)
+
+    def shared(n):
+        remote(send_buf.at[n], r_buf.at[n], SHARE + n, (g, t)).wait_recv()
+        return r_buf[n].astype(F32)
+
+    def project(b):
+        return jnp.dot(ctx_s[...], wo_s[b], preferred_element_type=F32)
+
+    share(0, project(far_twin), twin_t)
+    share(1, project(twin_t), twin_t)
+    far_sum = project(far_t) + shared(0)
+    share(2, far_sum, far_t)
+    own_sum = project(t) + shared(1)
+    share(3, own_sum, far_t)
     for w in both:
         w.second_forward(1)
-    for w in both:
-        w.second_forward(2)
-    for dt in (2, 1, 3):
-        remote(send_buf.at[dt - 1], r_buf.at[dt - 1], SHARE + dt - 1, (g, t)).wait_recv()
-    for i in range(3):
-        share = share + r_buf[i].astype(F32)
-    attended = share.astype(BF16)
+    from_far = shared(2)
+    also_far = shared(3)
+    attended = (own_sum + from_far).astype(BF16)
     att_out[...] = attended
     residual = (h_buf[t].astype(F32) + attended.astype(F32)).astype(BF16).astype(F32)
-    own_squares = jnp.sum(residual * residual, axis=1, keepdims=True)
+    far_attended = (far_sum + also_far).astype(BF16).astype(F32)
+    far_residual = (h_buf[far_t].astype(F32) + far_attended).astype(BF16).astype(F32)
+    own_squares = jnp.sum(residual * residual + far_residual * far_residual, axis=1, keepdims=True)
     stat_send[...] = jnp.broadcast_to(own_squares, (ROWS, HD))
-    stat_copies = []
-    for dt in (1, 2, 3):
-        c = remote(stat_send, stat_buf.at[dt - 1], STAT + dt - 1, (g, (t + dt) % 4))
-        c.start()
-        stat_copies.append(c)
-    for w in both:
-        w.second_far(0)
+    stat_copies = [remote(stat_send, stat_buf, STAT, (g, twin_t))]
+    stat_copies[0].start()
     for w in both:
         w.second_far(-1)
     for w in both:
         w.second_far(1)
-    for dt in (1, 2, 3):
-        remote(stat_send, stat_buf.at[dt - 1], STAT + dt - 1, (g, t)).wait_recv()
-    square_total = own_squares + stat_buf[0] + stat_buf[1] + stat_buf[2]
+    for w in both:
+        w.crossed()
+    remote(stat_send, stat_buf, STAT, (g, t)).wait_recv()
+    square_total = own_squares + stat_buf[...]
     inverse_post = lax.rsqrt(square_total * (1.0 / D) + EPS)
     for j in range(WIDTH // HD):
         gain = pg[pl.ds(t * (WIDTH // HD) + j, 1), :]
@@ -387,7 +450,7 @@
 
     for w in both:
         w.second_far(2)
-    for c in line_copies + hidden_copies + slice_copies + partial_copies + keys.started + values.started + share_copies + stat_copies:
+    for c in line_copies + hidden_copies + slice_copies + twin_copies + partial_copies + keys.started + values.started + share_copies + stat_copies:
         c.wait_send()
 
 
@@ -445,9 +508,9 @@
             pltpu.VMEM((ROWS, CACHE, HD), BF16),
             pltpu.VMEM((4, HEADS * HD, WIDTH), BF16),
             pltpu.VMEM((2, 4, ROWS, CHUNK), BF16),
-            pltpu.VMEM((4, ROWS, 2 * CHUNK), BF16),
             pltpu.VMEM((4, 2, ROWS, CHUNK), BF16),
-            pltpu.VMEM((4, ROWS, 2 * CHUNK), BF16),
+            pltpu.VMEM((4, 2, ROWS, CHUNK), BF16),
+            pltpu.VMEM((4, 2, ROWS, CHUNK), BF16),
             pltpu.VMEM((4, ROWS, HD), F32),
             pltpu.VMEM((4, ROWS, HD), F32),
             pltpu.VMEM((3, ROWS, HD), F32),
@@ -457,10 +520,10 @@
             pltpu.VMEM((ROWS, 8, HD), F32),
             pltpu.VMEM((ROWS, 8, HD), F32),
             pltpu.VMEM((ROWS, HEADS * HD), BF16),
-            pltpu.VMEM((3, ROWS, WIDTH), BF16),
-            pltpu.VMEM((3, ROWS, WIDTH), BF16),
+            pltpu.VMEM((4, ROWS, WIDTH), BF16),
+            pltpu.VMEM((4, ROWS, WIDTH), BF16),
             pltpu.VMEM((ROWS, HD), F32),
-            pltpu.VMEM((3, ROWS, HD), F32),
+            pltpu.VMEM((ROWS, HD), F32),
             pltpu.SemaphoreType.DMA((LOCALS,)),
             pltpu.SemaphoreType.DMA((COPIES,)),
             pltpu.SemaphoreType.DMA((COPIES,)),

time: 37.7 us -> 35.4 us (0.939)
  Pallas kernels: 36.9 us -> 34.6 us
    pallas_call x1, Pallas kernels: 35.4 us -> 33.1 us  [shards(): pl.pallas_call(kernel, out_shape=[pltpu.VMEM((ROWS, WIDTH), BF16), pltpu....]
where the time goes in v3:
time: 35.4 us; the launch traced here: 35.3 us
  Pallas kernels  34.6 us (98%)
  between operations  0.64 us (2%)
    pallas_call x1, Pallas kernels, shards(): pl.pallas_call(kernel, out_shape=[pltpu.VMEM((ROWS, WIDTH), BF16), pltpu....  33.1 us
    pallas_call x1, Pallas kernels, shards(): pl.pallas_call(store, out_shape=[jax.ShapeDtypeStruct(a.shape, a.dtype) f...  1.55 us

profile of v3, /device:TPU:1, one launch (start us, length us, event | category | flops | bytes accessed | tf_op | source)
XLA Modules:
  0.0 35.3 jit_solution(8292750636322330331)
XLA Ops:
  0.6 33.1 %decode.1 = (bf16[16,1280]{1,0:T(8,128)(2,1)S(1)}, bf16[16,1280]{1,0:T(8,128)(2,1)S(1)}, bf16[2,4,4,160,128]{4,3,2,1,0:T(8,128)(2,1)S(1)}, bf16[2,4,4,160,128]{4,3,2,1,0:T(8,128)(2,1)S(1)}) custom-call(bf16[16,1280]{1,0:T(8,128)(2,1)} %hid.1, s32[16]{0:T(128)} %lens.1, f32[40,128]{1,0:T(8,128)} %bitcast.13, f32[40,128]{1,0:T(8,128)} %bitcast.14, ...), custom_call_target="tpu_custom_call" | custom-call | tf_op jit(solution)/shard_map/decode/pallas_call | solution.py:487
  33.7 1.6 %store.1 = (bf16[16,1280]{1,0:T(8,128)(2,1)}, bf16[16,1280]{1,0:T(8,128)(2,1)}, bf16[5120,128]{1,0:T(8,128)(2,1)}, bf16[5120,128]{1,0:T(8,128)(2,1)}) custom-call(bf16[16,1280]{1,0:T(8,128)(2,1)S(1)} %get-tuple-element.8.refs_0_, bf16[16,1280]{1,0:T(8,128)(2,1)S(1)} %get-tuple-element.9.refs_1_, bf16[5120,128]{1,0:T(8,128)(2,1)S(1)} %bitcast.9, ...), custom_call_target="tpu_custom_call" | custom-call | tf_op jit(solution)/shard_map/store/pallas_call | solution.py:537

commit v4 on v3

--- a/solution.py
+++ b/solution.py
@@ -28,13 +28,15 @@
 
 HIDDEN = 0
 LINE = 3
-GATHER = 17
-SHARE = 63
-STAT = 67
-SLICE = 69
-TWIN = 75
-PARTIAL = 81
-COPIES = 87
+SHARE = 17
+STAT = 21
+SLICE = 22
+TWIN = 28
+PARTIAL = 34
+GATHER = 40
+EARLY = 9
+EACH = EARLY + 32
+COPIES = GATHER + 2 * EACH
 L_HID, L_LEN, L_IN, L_POST, L_BQ, L_BK, L_BV, L_OWNK, L_OWNV = range(9)
 L_WQ = 9
 L_KC = L_WQ + CHUNKS
@@ -81,9 +83,12 @@
     for c in small:
         c.start()
 
-    line = [(dx, dt) for dx in (1, 0) for dt in range(4) if (dx, dt) != (0, 0)]
+    lo, core = t // 2, t % 2
+    far_t, twin_t = (t + 2) % 4, t + 1 - 2 * core
+    far_twin = (twin_t + 2) % 4
+    line = [(xh, twin_t)] + [(1 - xh, b) for b in (t, twin_t, far_t, far_twin)] + [(xh, far_t), (xh, far_twin)]
     barrier = pltpu.get_barrier_semaphore()
-    partners = [(group((xh + dx) % 2, z, y), (t + dt) % 4) for dx, dt in line]
+    partners = [(group(a, z, y), b) for a, b in line]
     partners += [(group(xh, z, (y + d) % 4), t) for d in (1, 2, 3)]
     partners += [(group(xh, (z + d) % 4, y), t) for d in (1, 2, 3)]
     for dev in partners:
@@ -103,8 +108,6 @@
 
     pl.semaphore_wait(barrier, len(partners))
 
-    far_t, twin_t = (t + 2) % 4, t + 1 - 2 * (t % 2)
-    far_twin = (twin_t + 2) % 4
     hidden_copies = [
         remote(hid, h_buf.at[t], HIDDEN, (g, far_t)),
         remote(hid, h_buf.at[t], HIDDEN + 1, (g, twin_t)),
@@ -112,12 +115,10 @@
     for c in hidden_copies:
         c.start()
     line_copies = []
-    for n, (dx, dt) in enumerate(line):
-        to_t = (t + dt) % 4
-        dev = (group((xh + dx) % 2, z, y), to_t)
-        cols = pl.ds(pl.multiple_of(to_t * HD, HD), HD)
+    for n, (a, b) in enumerate(line):
+        cols = pl.ds(pl.multiple_of(b * HD, HD), HD)
         for kv, src in ((0, nk), (1, nv)):
-            c = remote(src.at[:, cols], x_buf.at[kv, xh, t], LINE + 2 * n + kv, dev)
+            c = remote(src.at[:, cols], x_buf.at[kv, xh, t], LINE + 2 * n + kv, (group(a, z, y), b))
             c.start()
             line_copies.append(c)
     def start_all(make, count):
@@ -146,6 +147,106 @@
 
     def rotate(v):
         return v * cosine + pltpu.roll(v, HD // 2, 1) * sine
+
+    class Gather:
+        def __init__(self, buf, first, second, at, base):
+            self.buf, self.a, self.b, self.at, self.base = buf, first, second, at, base
+            self.z, self.y = z, y
+            self.started = []
+
+        def slot(self, da, db, half=None):
+            p, q = (self.a + da + 4) % 4, (self.b + db + 4) % 4
+            zz, yy = self.at(p, q)
+            return self.buf.at[slice(None) if half is None else half, zz, yy]
+
+        def dev(self, da, db):
+            zz, yy = self.at((self.a + da + 4) % 4, (self.b + db + 4) % 4)
+            return (group(xh, zz, yy), t)
+
+        def send(self, src, i, da, db):
+            c = remote(src, src, self.base + i, self.dev(da, db))
+            c.start()
+            self.started.append(c)
+
+        def recv(self, land, i):
+            remote(land, land, self.base + i, (g, t)).wait_recv()
+
+        def first_own(self, n, half, rows):
+            mine = self.buf.at[half, self.z, self.y, rows]
+            for i, d in enumerate((2, 1, -1)):
+                self.send(mine, 3 * n + i, d, 0)
+
+        def first_all(self, n, half, rows):
+            for i, d in enumerate((2, 1, -1)):
+                zz, yy = self.at((self.a - d + 4) % 4, self.b)
+                self.recv(self.buf.at[half, zz, yy, rows], 3 * n + i)
+
+        def second(self, s, n, half, rows):
+            zz, yy = self.at((self.a + s + 4) % 4, self.b)
+            mine = self.buf.at[half, zz, yy, rows]
+            i = EARLY + 8 * (s % 4) + 2 * n
+            self.send(mine, i, 0, 1)
+            self.send(mine, i + 1, 0, -1)
+
+        def second_forward(self, s, blocks):
+            i = EARLY + 8 * (s % 4)
+            for d in (0, 1):
+                step = 2 * d - 1
+                zz, yy = self.at((self.a + s + 4) % 4, (self.b + step + 4) % 4)
+                for n, (half, rows) in enumerate(blocks):
+                    self.recv(self.buf.at[half, zz, yy, rows], i + 2 * n + d)
+                self.send(self.slot(s, step, d), i + 6 + d, 0, -step)
+
+        def second_far(self, s):
+            i = EARLY + 8 * (s % 4) + 6
+            self.recv(self.slot(s, 2, 0), i)
+            self.recv(self.slot(s, 2, 1), i + 1)
+
+    keys = Gather(k_out, y, z, lambda p, q: (q, p), GATHER)
+    values = Gather(v_out, z, y, lambda p, q: (p, q), GATHER + EACH)
+    both = (keys, values)
+
+    chip_rows = pl.ds(pl.multiple_of(lo * (BLOCK // 2), BLOCK // 2), BLOCK // 2)
+    next_rows = pl.ds(pl.multiple_of((1 - lo) * (BLOCK // 2), BLOCK // 2), BLOCK // 2)
+    own_blocks = ((xh, chip_rows), (xh, next_rows), (1 - xh, slice(None)))
+
+    def arrived(first, last):
+        for n in range(first, last):
+            for kv in (0, 1):
+                land = x_buf.at[kv, line[n][0], line[n][1]]
+                remote(land, land, LINE + 2 * n + kv, (g, t)).wait_recv()
+
+    def assemble(a, start, count, rows):
+        for kv, out in ((0, k_out), (1, v_out)):
+            block = x_buf[kv, a, pl.ds(start, count)].astype(F32).reshape(count * SHARD, HD).astype(BF16)
+            out[a, z, y, rows] = block
+
+    def first_own(n):
+        for w in both:
+            w.first_own(n, *own_blocks[n])
+
+    def first_all(n):
+        for w in both:
+            w.first_all(n, *own_blocks[n])
+
+    def second(s, n):
+        for w in both:
+            w.second(s, n, *own_blocks[n])
+
+    def second_forward(s):
+        for w in both:
+            w.second_forward(s, own_blocks)
+
+    def second_far(s):
+        for w in both:
+            w.second_far(s)
+
+    local(nk.at[:, columns], x_buf.at[0, xh, t], L_OWNK).wait()
+    local(nv.at[:, columns], x_buf.at[1, xh, t], L_OWNV).wait()
+    arrived(0, 1)
+    assemble(xh, 2 * lo, 2, chip_rows)
+    first_own(0)
+    second(0, 0)
 
     local(hid, h_buf.at[t], L_HID).wait()
     remote(hid, h_buf.at[far_t], HIDDEN, (g, t)).wait_recv()
@@ -174,7 +275,6 @@
             ).astype(BF16)
     nz_buf[z] = n_buf[:, z]
     ny_buf[y] = n2_buf[y]
-    core = t % 2
     slice_copies = []
     for d in (1, 2, 3):
         zz, yy = (z + d) % 4, (y + d) % 4
@@ -187,100 +287,14 @@
     for c in slice_copies:
         c.start()
 
-    local(nk.at[:, columns], x_buf.at[0, xh, t], L_OWNK).wait()
-    local(nv.at[:, columns], x_buf.at[1, xh, t], L_OWNV).wait()
-    for n, (dx, dt) in enumerate(line):
-        for kv, src in ((0, nk), (1, nv)):
-            land = x_buf.at[kv, (xh - dx + 2) % 2, (t - dt + 4) % 4]
-            remote(src.at[:, columns], land, LINE + 2 * n + kv, (g, t)).wait_recv()
-    for kv, out in ((0, k_out), (1, v_out)):
-        for i in (0, 1):
-            out[i, z, y] = x_buf[kv, i].astype(F32).reshape(BLOCK, HD).astype(BF16)
-
-    class Gather:
-        def __init__(self, buf, first, second, at, base):
-            self.buf, self.a, self.b, self.at, self.base = buf, first, second, at, base
-            self.started = []
-
-        def slot(self, da, db, half=None):
-            p, q = (self.a + da + 4) % 4, (self.b + db + 4) % 4
-            zz, yy = self.at(p, q)
-            return self.buf.at[slice(None) if half is None else half, zz, yy]
-
-        def dev(self, da, db):
-            zz, yy = self.at((self.a + da + 4) % 4, (self.b + db + 4) % 4)
-            return (group(xh, zz, yy), t)
-
-        def send(self, src, i, da, db):
-            c = remote(src, src, self.base + i, self.dev(da, db))
-            c.start()
-            self.started.append(c)
-
-        def recv(self, land, i):
-            remote(land, land, self.base + i, (g, t)).wait_recv()
-
-        def first_own(self):
-            for i, d in enumerate((1, -1, 2)):
-                self.send(self.slot(0, 0), i, d, 0)
-
-        def first_near(self):
-            self.recv(self.slot(-1, 0), 0)
-            self.recv(self.slot(1, 0), 1)
-
-        def first_far(self):
-            self.recv(self.slot(2, 0), 2)
-
-        def second(self, s):
-            half = xh if s == 0 else None
-            self.send(self.slot(s, 0, half), 4 + 4 * (s % 4), 0, 1)
-            self.send(self.slot(s, 0, half), 5 + 4 * (s % 4), 0, -1)
-            if s == 2:
-                self.send(self.slot(2, 0), 14, 0, 2)
-
-        def piece(self, s, db, part):
-            if s == 0:
-                return self.slot(0, db, xh).at[pl.ds(part * (BLOCK // 2), BLOCK // 2)]
-            return self.slot(s, db, part)
-
-        def second_forward(self, s):
-            i = 4 + 4 * (s % 4)
-            half = xh if s == 0 else None
-            self.recv(self.slot(s, -1, half), i)
-            self.send(self.piece(s, -1, 0), i + 2, 0, 1)
-            self.recv(self.slot(s, 1, half), i + 1)
-            self.send(self.piece(s, 1, 1), i + 3, 0, -1)
-
-        def second_far(self, s):
-            i = 4 + 4 * (s % 4)
-            if s == 2:
-                for k, db in enumerate((-1, 1, 2)):
-                    self.recv(self.slot(2, db), i + k)
-                return
-            self.recv(self.piece(s, 2, 0), i + 2)
-            self.recv(self.piece(s, 2, 1), i + 3)
-
-        def cross(self, i, db):
-            half = self.slot(0, db, xh)
-            c = remote(half, half, self.base + 20 + i, (group(1 - xh, z, y), t))
-            c.start()
-            self.started.append(c)
-
-        def cross_near(self):
-            self.cross(0, -1)
-            self.cross(1, 1)
-
-        def cross_far(self):
-            self.cross(2, 2)
-
-        def crossed(self):
-            for i, db in enumerate((-1, 1, 2)):
-                self.recv(self.slot(0, db, 1 - xh), 20 + i)
-
-    keys = Gather(k_out, y, z, lambda p, q: (q, p), GATHER)
-    values = Gather(v_out, z, y, lambda p, q: (p, q), GATHER + 23)
-    both = (keys, values)
-    for w in both:
-        w.first_own()
+    arrived(1, 5)
+    assemble(1 - xh, 0, 4, slice(None))
+    first_own(2)
+    arrived(5, 7)
+    assemble(xh, 2 * (1 - lo), 2, next_rows)
+    first_own(1)
+    second(0, 2)
+    second(0, 1)
 
     for i in range(CHUNKS):
         wq_copy(i).wait()
@@ -292,8 +306,9 @@
         v = rotate(total[:, h * HD : (h + 1) * HD] + bq_s[h : h + 1, :])
         q_s[:, h, :] = v.astype(BF16).astype(F32)
 
-    for w in both:
-        w.second(0)
+    first_all(0)
+    for s in (2, -1, 1):
+        second(s, 0)
 
     upper = lax.broadcasted_iota(jnp.int32, (16, 1), 0) < 8
     slot_ids = lax.broadcasted_iota(jnp.int32, (16, CACHE), 1)
@@ -333,13 +348,9 @@
             c = remote(land, land, TWIN + i, (g, twin_t))
             c.start()
             twin_copies.append(c)
-    for w in both:
-        w.first_near()
-    for w in both:
-        w.second(-1)
     attend_twice(2, 0)
-    for w in both:
-        w.first_far()
+    first_all(2)
+    first_all(1)
     for d in (1, 2, 3):
         zz, yy = (z - d + 4) % 4, (y - d + 4) % 4
         theirs = nz_buf.at[zz, 1 - core]
@@ -365,22 +376,12 @@
         partial_copies.append(remote(pv_send.at[yy], pv_buf.at[d - 1], PARTIAL + d + 2, (group(xh, z, yy), t)))
     for c in partial_copies:
         c.start()
-    for w in both:
-        w.second_forward(0)
-    for w in both:
-        w.cross_near()
-    for w in both:
-        w.second(1)
-    for w in both:
-        w.second(2)
+    for s in (2, -1, 1):
+        second(s, 2)
+        second(s, 1)
     attend_twice(3, 0)
-
-    for w in both:
-        w.second_far(0)
-    for w in both:
-        w.cross_far()
-    for w in both:
-        w.second_forward(-1)
+    second_forward(0)
+
 
     for d in (1, 2, 3):
         remote(pk_send.at[z], pk_buf.at[d - 1], PARTIAL + d - 1, (g, t)).wait_recv()
@@ -418,12 +419,13 @@
 
     share(0, project(far_twin), twin_t)
     share(1, project(twin_t), twin_t)
+    second_forward(2)
     far_sum = project(far_t) + shared(0)
     share(2, far_sum, far_t)
     own_sum = project(t) + shared(1)
     share(3, own_sum, far_t)
-    for w in both:
-        w.second_forward(1)
+    second_forward(-1)
+    second_forward(1)
     from_far = shared(2)
     also_far = shared(3)
     attended = (own_sum + from_far).astype(BF16)
@@ -435,12 +437,8 @@
     stat_send[...] = jnp.broadcast_to(own_squares, (ROWS, HD))
     stat_copies = [remote(stat_send, stat_buf, STAT, (g, twin_t))]
     stat_copies[0].start()
-    for w in both:
-        w.second_far(-1)
-    for w in both:
-        w.second_far(1)
-    for w in both:
-        w.crossed()
+    for s in (0, 2, -1):
+        second_far(s)
     remote(stat_send, stat_buf, STAT, (g, t)).wait_recv()
     square_total = own_squares + stat_buf[...]
     inverse_post = lax.rsqrt(square_total * (1.0 / D) + EPS)
@@ -448,8 +446,7 @@
         gain = pg[pl.ds(t * (WIDTH // HD) + j, 1), :]
         norm_out[:, j * HD : (j + 1) * HD] = (residual[:, j * HD : (j + 1) * HD] * inverse_post * gain).astype(BF16)
 
-    for w in both:
-        w.second_far(2)
+    second_far(1)
     for c in line_copies + hidden_copies + slice_copies + twin_copies + partial_copies + keys.started + values.started + share_copies + stat_copies:
         c.wait_send()
 

time: 35.4 us -> 34.4 us (0.972)
  Pallas kernels: 34.6 us -> 33.7 us
    pallas_call x1, Pallas kernels: 33.1 us -> 32.1 us  [shards(): pl.pallas_call(kernel, out_shape=[pltpu.VMEM((ROWS, WIDTH), BF16), pltpu....]
where the time goes in v4:
time: 34.4 us; the launch traced here: 34.3 us
  Pallas kernels  33.7 us (98%)
  between operations  0.64 us (2%)
    pallas_call x1, Pallas kernels, shards(): pl.pallas_call(kernel, out_shape=[pltpu.VMEM((ROWS, WIDTH), BF16), pltpu....  32.1 us
    pallas_call x1, Pallas kernels, shards(): pl.pallas_call(store, out_shape=[jax.ShapeDtypeStruct(a.shape, a.dtype) f...  1.55 us

profile of v4, /device:TPU:1, one launch (start us, length us, event | category | flops | bytes accessed | tf_op | source)
XLA Modules:
  0.0 34.3 jit_solution(17134749711476323625)
XLA Ops:
  0.6 32.1 %decode.1 = (bf16[16,1280]{1,0:T(8,128)(2,1)S(1)}, bf16[16,1280]{1,0:T(8,128)(2,1)S(1)}, bf16[2,4,4,160,128]{4,3,2,1,0:T(8,128)(2,1)S(1)}, bf16[2,4,4,160,128]{4,3,2,1,0:T(8,128)(2,1)S(1)}) custom-call(bf16[16,1280]{1,0:T(8,128)(2,1)} %hid.1, s32[16]{0:T(128)} %lens.1, f32[40,128]{1,0:T(8,128)} %bitcast.13, f32[40,128]{1,0:T(8,128)} %bitcast.14, ...), custom_call_target="tpu_custom_call" | custom-call | tf_op jit(solution)/shard_map/decode/pallas_call | solution.py:484
  32.8 1.6 %store.1 = (bf16[16,1280]{1,0:T(8,128)(2,1)}, bf16[16,1280]{1,0:T(8,128)(2,1)}, bf16[5120,128]{1,0:T(8,128)(2,1)}, bf16[5120,128]{1,0:T(8,128)(2,1)}) custom-call(bf16[16,1280]{1,0:T(8,128)(2,1)S(1)} %get-tuple-element.8.refs_0_, bf16[16,1280]{1,0:T(8,128)(2,1)S(1)} %get-tuple-element.9.refs_1_, bf16[5120,128]{1,0:T(8,128)(2,1)S(1)} %bitcast.9, ...), custom_call_target="tpu_custom_call" | custom-call | tf_op jit(solution)/shard_map/store/pallas_call | solution.py:534
